TPU v7x, 32 devices: a whole 2x2x4 slice. The times are simulated.
32 devices in a mesh: view: 8 (over z, y), depth: 4 (over x, core).
Axes of the slice: x: 2, y: 2, z: 4, core: 2. Of those that a mesh axis runs over, the one named last changes fastest.
Arguments:
- features: bfloat16 [24, 1024, 32], P('view'), may hold values from -6 to 6
- view_lists: int32 [24, 10], P('view'), may hold values from 0 to 15
- requests: int32 [8, 8, 2], replicated, may hold values from 0 to 2
- warp_idx: int32 [24, 10, 64, 8, 128], P('view', None, None, 'depth'), may hold values from -682 to 1023
- conv_weight: bfloat16 [27, 8, 8], replicated, may hold values from -0.4375 to 0.4375
Outputs:
- regularized: bfloat16 [24, 8, 64, 8, 128], P('view', None, 'depth')
Inputs may be any that keep to these rules, and one draw needn't show every extreme that they name: `warp_idx`: A negative entry marks a sample that falls outside the source tile and is left out of the sum and the count.
All inputs are finite; a program needn't handle non-finite values.
Results may differ from a plain program's by a relative error of at most 0.0049.
Values may be sent and summed in bfloat16 or wider, within the bound.
A program may use at most 128 MiB of HBM per device.

v0:
```python
import jax
import jax.numpy as jnp
from jax import lax
from jax.sharding import PartitionSpec as P


def padded_2(cells, sides, width):
    for axis, dim in sides:
        count = lax.axis_size(axis)
        ends = count - 1
        head = lax.slice_in_dim(cells, 0, width, axis=dim)
        tail = lax.slice_in_dim(cells, cells.shape[dim] - width, cells.shape[dim], axis=dim)
        cells = jnp.concatenate(
            [
                lax.ppermute(tail, axis, [(i, (i + 1) % count) for i in range(ends)]),
                cells,
                lax.ppermute(head, axis, [((i + 1) % count, i) for i in range(ends)]),
            ],
            axis=dim,
        )
    return cells


def mix_taps(padded, conv_weight, depth_out, rows_out, cols_out):
    summed = None
    for depth_tap in range(3):
        for row_tap in range(3):
            for col_tap in range(3):
                shifted = padded[
                    :,
                    :,
                    depth_tap : depth_tap + depth_out,
                    row_tap : row_tap + rows_out,
                    col_tap : col_tap + cols_out,
                ]
                kernel = conv_weight[9 * depth_tap + 3 * row_tap + col_tap]
                term = jnp.einsum(
                    "vgdhw,gk->vkdhw", shifted, kernel, preferred_element_type=jnp.float32
                )
                summed = term if summed is None else summed + term
    return summed


def on_device(features, view_lists, requests, warp_idx, conv_weight):
    view_here = lax.axis_index("view")
    depth_here = lax.axis_index("depth")
    view_count = lax.axis_size("view")
    depth_count = lax.axis_size("depth")
    pixels = features.shape[1]
    channels = features.shape[2]
    sources = warp_idx.shape[1]
    planes = warp_idx.shape[2]
    row_count = warp_idx.shape[3]
    columns = warp_idx.shape[4]
    groups = conv_weight.shape[1]
    asked = requests.shape[2]
    wanted = requests[:, view_here, :].reshape(-1)
    outgoing = jnp.take(features, wanted, axis=0).reshape(view_count, asked, pixels, channels)
    tile_pool = lax.all_to_all(outgoing, "view", split_axis=0, concat_axis=0, tiled=True)
    flat_pool = tile_pool.reshape(-1, channels)
    own_pixels = row_count * columns
    own_rows = lax.dynamic_slice_in_dim(features, depth_here * own_pixels, own_pixels, 1)

    def one_view(item):
        own_tile, warp_rows, view_sources = item
        usable = (warp_rows >= 0).reshape(sources, planes, own_pixels)
        picks = view_sources[:, None, None, None] * pixels + jnp.maximum(warp_rows, 0)
        warped = jnp.take(flat_pool, picks.reshape(-1), axis=0)
        warped = warped.reshape(sources, planes, own_pixels, groups, channels // groups)
        own_groups = own_tile.reshape(own_pixels, groups, channels // groups)
        products = jnp.einsum(
            "sdpgk,pgk->sdpg", warped, own_groups, preferred_element_type=jnp.float32
        )
        masked = jnp.where(usable[..., None], products, jnp.float32(0.0))
        live_count = jnp.sum(usable.astype(jnp.float32), axis=0)
        corr = 0.5 * jnp.sum(masked, axis=0) / jnp.maximum(live_count, jnp.float32(1.0))[..., None]
        corr = jnp.transpose(corr, (2, 0, 1)).reshape(groups, planes, row_count, columns)
        return corr.astype(jnp.bfloat16)

    cost_rows = lax.map(one_view, (own_rows, warp_idx, view_lists))
    slab_planes = planes // depth_count
    slab = lax.all_to_all(cost_rows, "depth", split_axis=2, concat_axis=3, tiled=True)
    rimmed = padded_2(slab, (("depth", 2),), 1)
    rimmed = jnp.pad(rimmed, ((0, 0), (0, 0), (0, 0), (1, 1), (1, 1)))
    summed = mix_taps(rimmed, conv_weight, slab_planes, row_count * depth_count, columns)
    return summed.astype(jnp.bfloat16)


def solution(mesh):
    return jax.shard_map(
        on_device,
        mesh=mesh,
        in_specs=(
            P("view", None, None),
            P("view", None),
            P(),
            P("view", None, None, "depth", None),
            P(),
        ),
        out_specs=P("view", None, "depth", None, None),
        check_vma=False,
    )
```

profile of v0, /device:TPU:1, one launch (start us, length us, event | category | flops | bytes accessed | tf_op | source)
XLA Modules:
  0.0 1940.4 jit_solution(3619207925280772178)
XLA Ops:
  3.1 6.4 all-to-all-start
  9.5 24.6 %all-to-all-done = bf16[8,2,1024,32]{2,3,1,0:T(8,128)(2,1)S(1)} async-done(((bf16[8,2,1024,32]{2,3,1,0:T(8,128)(2,1)}), bf16[8,2,1024,32]{2,3,1,0:T(8,128)(2,1)S(1)}, u32[]{:S(2)}, u32[]{:S(2)}) %all-to-all-start) | async-done | bytes 1048608 | tf_op jit(solution)/shard_map/all_to_all | solution.py:59
  34.1 3.1 copy.344
  37.2 1826.4 %while.10 = (s32[]{:T(128)}, bf16[3,8,64,2,128]{4,3,1,0,2:T(2,128)(2,1)}, s32[3,10,64,2,128]{4,3,2,1,0:T(2,128)S(1)}, bf16[3,256,32]{1,2,0:T(8,128)(2,1)S(1)}, s...) while((s32[]{:T(128)}, bf16[3,8,64,2,128]{4,3,1,0,2:T(2,128)(2,1)}, ...), condition=%wide.region_3.4_spmd, body=%wide.region_0.3_spmd.sunk | while | flops 25174028 | bytes 96813416 | solution.py:80
  42.2 545.8 %gather_fusion = bf16[163840,32]{1,0:T(8,128)(2,1)} fusion(bf16[16384,32]{1,0:T(8,128)(2,1)} %get-tuple-element.155, s32[163840]{0:T(1024)S(1)} %broadcast_clamp_fusion.2), kind=kCustom, calls=%fused_computation.clone.1 | custom fusion | bytes 21626880 | tf_op jit(solution)/shard_map/while/body/eval_jaxpr/jit(_take)/gather | solution.py:68
  588.0 33.0 %copy.425 = bf16[163840,32]{0,1:T(8,128)(2,1)} copy(bf16[163840,32]{1,0:T(8,128)(2,1)} %gather_fusion) | data formatting | bytes 20971520 | tf_op jit(solution)/shard_map/while/body/eval_jaxpr/jit(_take)/gather | solution.py:68
  621.0 10.5 copy.426
  631.5 10.1 multiply_reduce_fusion.2
  641.6 3.1 fusion.108
  651.0 545.8 %gather_fusion = bf16[163840,32]{1,0:T(8,128)(2,1)} fusion(bf16[16384,32]{1,0:T(8,128)(2,1)} %get-tuple-element.155, s32[163840]{0:T(1024)S(1)} %broadcast_clamp_fusion.2), kind=kCustom, calls=%fused_computation.clone.1 | custom fusion | bytes 21626880 | tf_op jit(solution)/shard_map/while/body/eval_jaxpr/jit(_take)/gather | solution.py:68
  1196.8 33.0 %copy.425 = bf16[163840,32]{0,1:T(8,128)(2,1)} copy(bf16[163840,32]{1,0:T(8,128)(2,1)} %gather_fusion) | data formatting | bytes 20971520 | tf_op jit(solution)/shard_map/while/body/eval_jaxpr/jit(_take)/gather | solution.py:68
  1229.8 10.5 copy.426
  1240.3 10.1 multiply_reduce_fusion.2
  1250.4 3.1 fusion.108
  1259.8 545.8 %gather_fusion = bf16[163840,32]{1,0:T(8,128)(2,1)} fusion(bf16[16384,32]{1,0:T(8,128)(2,1)} %get-tuple-element.155, s32[163840]{0:T(1024)S(1)} %broadcast_clamp_fusion.2), kind=kCustom, calls=%fused_computation.clone.1 | custom fusion | bytes 21626880 | tf_op jit(solution)/shard_map/while/body/eval_jaxpr/jit(_take)/gather | solution.py:68
  1805.6 33.0 %copy.425 = bf16[163840,32]{0,1:T(8,128)(2,1)} copy(bf16[163840,32]{1,0:T(8,128)(2,1)} %gather_fusion) | data formatting | bytes 20971520 | tf_op jit(solution)/shard_map/while/body/eval_jaxpr/jit(_take)/gather | solution.py:68
  1838.6 10.5 copy.426
  1849.1 10.1 multiply_reduce_fusion.2
  1859.2 3.1 fusion.108
  1863.6 5.9 all-to-all-start.1
  1873.4 6.9 all-to-all-done.1
  1880.5 2.7 collective-permute-start
  1883.2 1.9 collective-permute-start.1
  1885.6 3.0 collective-permute-done.1
  1888.7 2.0 select_maximum_fusion
  1891.9 1.6 fusion.28
  1893.5 1.6 fusion.30
  1895.1 1.6 fusion.32
  1896.7 1.6 fusion.34
  1898.3 1.7 fusion.36
  1899.9 1.6 fusion.38
  1901.6 1.6 fusion.40
  1903.1 1.6 fusion.42
  1904.8 1.6 fusion.44
  1906.3 1.6 fusion.46
  1907.9 1.6 fusion.48
  1909.5 1.6 fusion.50
  1911.1 1.6 fusion.52
  1912.7 1.7 fusion.54
  1914.3 1.6 fusion.56
  1915.9 1.7 fusion.58
  1917.6 1.6 fusion.60
  1919.2 1.6 fusion.62
  1920.8 1.6 fusion.64
  1922.4 1.6 fusion.66
  1923.9 1.6 fusion.17
  1925.5 1.6 fusion.13
  1927.1 12.3 fusion.12
  (122 shorter events, 28.6 us)
Async XLA Ops:
  0.0 1.3 copy-start
  3.1 31.0 %all-to-all-start = ((bf16[8,2,1024,32]{2,3,1,0:T(8,128)(2,1)}), bf16[8,2,1024,32]{2,3,1,0:T(8,128)(2,1)S(1)}, u32[]{:S(2)}, u32[]{:S(2)}) async-start(bf16[8,2,1024,32]{2,3,1,0:T(8,128)(2,1)} %broadcast_select_fusion), calls=%async_computation | async-start | bytes 2097152 | tf_op jit(solution)/shard_map/all_to_all | solution.py:59
  9.5 27.7 %copy-start.2 = (s32[3,10,64,2,128]{4,3,2,1,0:T(2,128)S(1)}, s32[3,10,64,2,128]{4,3,2,1,0:T(2,128)}, u32[]{:S(2)}) copy-start(s32[3,10,64,2,128]{4,3,2,1,0:T(2,128)} %param.10) | copy-start | bytes 5898244
  37.2 2.9 copy-start.5
  631.5 10.1 copy-start.3
  641.6 4.4 copy-start.6
  646.0 2.9 copy-start.5
  1240.3 10.1 copy-start.3
  1250.4 4.4 copy-start.6
  1254.8 2.9 copy-start.5
  1849.1 10.1 copy-start.3
  1859.2 4.4 copy-start.6
  1863.6 5.9 copy-start.4
  1863.6 16.7 all-to-all-start.1
  1880.5 5.1 collective-permute-start
  1883.2 5.4 collective-permute-start.1
  1927.1 13.3 copy-start.1
where the time goes:
time: 1940 us
  local copies, waits for them, and re-layouts  1790 us (92%)
  other arithmetic  53 us (3%)
  matrix products  49.1 us (3%)
  waiting for transfers between devices  34.5 us (2%)
    gather x6, local copies, waits for them, and re-layouts, one_view(): warped = jnp.take(flat_pool, picks.reshape(-1), axis=0)  1740 us
    dot_general x27, matrix products, mix_taps(): jnp.einsum('vgdhw,gk->vkdhw', shifted, kernel, preferred_element_type=jnp...  49.1 us
  transfers between devices with their start and end apart: 4, of which 3 were waited for; matrix products, arithmetic and copies ran while one was open for 0% of the time, Pallas kernels for 0%

commit v1 on v0

v1 whole, which is shorter than its diff:
```python
import functools

import jax
import jax.numpy as jnp
import numpy as np
from jax import lax
from jax.experimental import pallas as pl
from jax.experimental.pallas import tpu as pltpu
from jax.sharding import PartitionSpec as P

LOW = 256


def cost_kernel(sources, high, kinds, groups, source_ref, idx_ref, pool_ref, own_ref, out_ref):
    view = pl.program_id(0)
    columns = idx_ref.shape[-1]
    pairs = idx_ref.shape[2] // 2
    chans = kinds * groups
    iota = lax.broadcasted_iota(jnp.int32, (16, columns), 0).astype(jnp.float32)
    one = jnp.ones((16, columns), jnp.bfloat16)
    zero = jnp.zeros((16, columns), jnp.bfloat16)
    steps = [(iota + float(16 * m)).astype(jnp.bfloat16) for m in range(LOW // 16)]

    def one_pair(pair, carry):
        total = [jnp.zeros((groups, columns), jnp.float32) for _ in range(2)]
        live = [jnp.zeros((groups, columns), jnp.float32) for _ in range(2)]
        for k in range(sources):
            hots, highs = [], []
            for q in range(2):
                row = idx_ref[0, k, pl.ds(2 * pair + q, 1), :]
                row = jnp.broadcast_to(row, (groups, columns))
                usable = row >= 0
                live[q] = live[q] + jnp.where(usable, 1.0, 0.0)
                low = jnp.where(usable, row & (LOW - 1), -1).astype(jnp.float32)
                low = jnp.concatenate([low, low], axis=0).astype(jnp.bfloat16)
                hots.append(
                    jnp.concatenate([jnp.where(s == low, one, zero) for s in steps], axis=0)
                )
                highs.append(row)
            table = pool_ref[source_ref[view * sources + k]]
            found = jnp.dot(
                table, jnp.concatenate(hots, axis=1), preferred_element_type=jnp.float32
            )
            for q in range(2):
                bits = []
                width = LOW
                while width < LOW * high:
                    bits.append((highs[q] & width) != 0)
                    width *= 2
                for t in range(kinds):
                    parts = [
                        found[
                            h * chans + t * groups : h * chans + (t + 1) * groups,
                            q * columns : (q + 1) * columns,
                        ]
                        for h in range(high)
                    ]
                    for bit in bits:
                        parts = [
                            jnp.where(bit, parts[2 * i + 1], parts[2 * i])
                            for i in range(len(parts) // 2)
                        ]
                    own = own_ref[0, t * groups : (t + 1) * groups, q * columns : (q + 1) * columns]
                    total[q] = total[q] + parts[0] * own
        cost = [0.5 * total[q] / jnp.maximum(live[q], 1.0) for q in range(2)]
        start = pl.multiple_of(pair * 2 * groups, 2 * groups)
        out_ref[0, pl.ds(start, 2 * groups), :] = jnp.concatenate(cost, axis=0).astype(jnp.bfloat16)
        return carry

    lax.fori_loop(0, pairs, one_pair, 0)


def conv_kernel(planes, groups, rows, slab_ref, band_ref, out_ref):
    shares = slab_ref.shape[0]
    columns = slab_ref.shape[-1]
    height = slab_ref.shape[2] // (planes + 2)
    out_rows = groups * rows
    lane = lax.broadcasted_iota(jnp.int32, (out_rows, columns), 1)
    for first in range(0, planes, 2):
        block = jnp.concatenate(
            [
                jnp.concatenate(
                    [slab_ref[s, 0, p * height : (p + 3) * height, :] for s in range(shares)],
                    axis=0,
                )
                for p in (first, first + 1)
            ],
            axis=1,
        )
        mixed = jnp.dot(band_ref[...], block, preferred_element_type=jnp.float32)
        for q in range(2):
            part = mixed[:, q * columns : (q + 1) * columns]
            left = pltpu.roll(part[:out_rows], 1, 1)
            right = pltpu.roll(part[2 * out_rows :], columns - 1, 1)
            total = part[out_rows : 2 * out_rows]
            total = total + jnp.where(lane == 0, 0.0, left)
            total = total + jnp.where(lane == columns - 1, 0.0, right)
            total = total.astype(jnp.bfloat16)
            for h in range(groups):
                out_ref[0, h, first + q] = total[h * rows : (h + 1) * rows]


def on_device(features, view_lists, requests, warp_idx, conv_weight):
    view_here = lax.axis_index("view")
    depth_here = lax.axis_index("depth")
    view_count = lax.axis_size("view")
    depth_count = lax.axis_size("depth")
    views, pixels, channels = features.shape
    sources, planes, row_count, columns = warp_idx.shape[1:]
    groups = conv_weight.shape[1]
    kinds = channels // groups
    high = pixels // LOW
    asked = requests.shape[2]
    rows = row_count * depth_count

    tables = features.reshape(views, high, LOW, groups, kinds).transpose(0, 1, 4, 3, 2)
    tables = tables.reshape(views, high * channels, LOW)
    wanted = requests[:, view_here, :].reshape(-1)
    outgoing = jnp.take(tables, wanted, axis=0).reshape(view_count, asked, high * channels, LOW)
    pool = lax.all_to_all(outgoing, "view", split_axis=0, concat_axis=0, tiled=True)
    pool = pool.reshape(view_count * asked, high * channels, LOW)

    own_pixels = row_count * columns
    own = lax.dynamic_slice_in_dim(features, depth_here * own_pixels, own_pixels, 1)
    own = own.reshape(views, own_pixels, groups, kinds).transpose(0, 3, 2, 1)
    own = own.reshape(views, channels, own_pixels).astype(jnp.float32)
    if row_count == 1:
        own = jnp.concatenate([own, own], axis=2)
    idx = warp_idx.reshape(views, sources, planes * row_count, columns)

    cost = pl.pallas_call(
        functools.partial(cost_kernel, sources, high, kinds, groups),
        grid_spec=pltpu.PrefetchScalarGridSpec(
            num_scalar_prefetch=1,
            grid=(views,),
            in_specs=[
                pl.BlockSpec((1, sources, planes * row_count, columns), lambda v, s: (v, 0, 0, 0)),
                pl.BlockSpec(pool.shape, lambda v, s: (0, 0, 0)),
                pl.BlockSpec((1,) + own.shape[1:], lambda v, s: (v, 0, 0)),
            ],
            out_specs=pl.BlockSpec(
                (1, planes * row_count * groups, columns), lambda v, s: (v, 0, 0)
            ),
        ),
        out_shape=jax.ShapeDtypeStruct(
            (views, planes * row_count * groups, columns), jnp.bfloat16
        ),
        compiler_params=pltpu.CompilerParams(vmem_limit_bytes=40 * 1024 * 1024),
    )(view_lists.reshape(-1), idx, pool, own)

    height = row_count * groups
    slab_planes = planes // depth_count
    padded = jnp.pad(cost, ((0, 0), (height, height), (0, 0)))
    slabs = jnp.stack(
        [
            lax.slice_in_dim(
                padded, t * slab_planes * height, ((t + 1) * slab_planes + 2) * height, axis=1
            )
            for t in range(depth_count)
        ]
    )
    slabs = lax.all_to_all(slabs, "depth", split_axis=0, concat_axis=0, tiled=True)

    place = np.zeros((rows, depth_count, row_count, 3), np.float32)
    for i in range(rows):
        for b in range(3):
            j = i + b - 1
            if 0 <= j < rows:
                place[i, j // row_count, j % row_count, b] = 1.0
    taps = conv_weight.reshape(3, 3, 3, groups, groups)
    band = jnp.einsum(
        "abegh,isrb->ehisarg",
        taps,
        jnp.asarray(place, jnp.bfloat16),
        preferred_element_type=jnp.float32,
    ).astype(jnp.bfloat16)
    band = band.reshape(3 * groups * rows, depth_count * 3 * height)

    return pl.pallas_call(
        functools.partial(conv_kernel, slab_planes, groups, rows),
        grid=(views,),
        in_specs=[
            pl.BlockSpec(
                (depth_count, 1, (slab_planes + 2) * height, columns), lambda v: (0, v, 0, 0)
            ),
            pl.BlockSpec(band.shape, lambda v: (0, 0)),
        ],
        out_specs=pl.BlockSpec(
            (1, groups, slab_planes, rows, columns), lambda v: (v, 0, 0, 0, 0)
        ),
        out_shape=jax.ShapeDtypeStruct(
            (views, groups, slab_planes, rows, columns), jnp.bfloat16
        ),
        compiler_params=pltpu.CompilerParams(vmem_limit_bytes=32 * 1024 * 1024),
    )(slabs, band)


def solution(mesh):
    return jax.shard_map(
        on_device,
        mesh=mesh,
        in_specs=(
            P("view", None, None),
            P("view", None),
            P(),
            P("view", None, None, "depth", None),
            P(),
        ),
        out_specs=P("view", None, "depth", None, None),
        check_vma=False,
    )
```

time: 1940 us -> 129 us (0.07)
  local copies, waits for them, and re-layouts: 1790 us -> 5.73 us
  Pallas kernels: 0 us -> 73.4 us
  other arithmetic: 53 us -> 3 us
  matrix products: 49.1 us -> 0.52 us
    gather x7 -> x1, local copies, waits for them, and re-layouts: 1740 us -> 0.61 us  [on_device(): jnp.take(tables, wanted, axis=0)]
    pallas_call x0 -> x2, Pallas kernels: none -> 73.4 us  [the longest x1 70.9 us: on_device(): pl.pallas_call(functools.partial(cost_kernel, sources, high, kinds, group...]
    dot_general x27 -> x1, matrix products: 49.1 us -> 0.52 us  [on_device(): jnp.einsum('abegh,isrb->ehisarg', taps, jnp.asarray(place, jnp.bfloat16),...]
    while x25 -> x0, local copies, waits for them, and re-layouts: 34.6 us -> none
    dot_general x3 -> x0, other arithmetic: 30.2 us -> none  [one_view(): jnp.einsum('sdpgk,pgk->sdpg', warped, own_groups, preferred_element_type=...]
  transfers between devices with their start and end apart: 4 -> 2, of which waited for: 3 -> 2; matrix products, arithmetic and copies ran while one was open for 0% -> 3% of each run, Pallas kernels for 0% -> 0%
where the time goes in v1:
time: 129 us; the launch traced here: 127 us
  Pallas kernels  73.4 us (57%)
  waiting for transfers between devices  32.4 us (25%)
  starting transfers between devices  12.2 us (9%)
  local copies, waits for them, and re-layouts  5.73 us (4%)
  other arithmetic  3 us (2%)
    pallas_call x1, Pallas kernels, on_device(): pl.pallas_call(functools.partial(cost_kernel, sources, high, kinds, group...  70.9 us
    all_to_all x1, waiting for transfers between devices, on_device(): lax.all_to_all(outgoing, 'view', split_axis=0, concat_axis=0, tiled=True)  23.6 us
    all_to_all x1, waiting for transfers between devices, on_device(): lax.all_to_all(slabs, 'depth', split_axis=0, concat_axis=0, tiled=True)  8.76 us
    all_to_all x1, starting transfers between devices, on_device(): lax.all_to_all(outgoing, 'view', split_axis=0, concat_axis=0, tiled=True)  6.51 us
    all_to_all x1, starting transfers between devices, on_device(): lax.all_to_all(slabs, 'depth', split_axis=0, concat_axis=0, tiled=True)  5.7 us
  transfers between devices with their start and end apart: 2, of which 2 were waited for; matrix products, arithmetic and copies ran while one was open for 3% of the time, Pallas kernels for 0%

profile of v1, /device:TPU:1, one launch (start us, length us, event | category | flops | bytes accessed | tf_op | source)
XLA Modules:
  0.0 127.3 jit_solution(10822847405175364727)
XLA Ops:
  0.0 1.0 fusion.5
  1.0 0.1 reshape_squeeze.6
  1.1 0.1 copy.18
  1.2 0.1 copy.19
  1.3 1.1 reshape.67
  2.3 0.1 copy.20
  2.4 0.6 gather_fusion
  3.0 1.1 broadcast_select_fusion
  4.2 0.0 copy-start.3
  4.2 0.0 copy-start
  4.2 6.5 %all-to-all-start = ((bf16[8,2,128,256]{3,2,1,0:T(8,128)(2,1)}), bf16[8,2,128,256]{3,2,1,0:T(8,128)(2,1)S(1)}, u32[]{:S(2)}, u32[]{:S(2)}) async-start(bf16[8,2,128,256]{3,2,1,0:T(8,128)(2,1)} %broadcast_select_fusion), calls=%async_computation | async-start | bytes 2097152 | tf_op jit(solution)/shard_map/all_to_all | solution.py:120
  10.7 0.0 copy-done.3
  10.7 0.1 reshape.65.source_ref
  10.8 0.8 dynamic-slice_convert_fusion
  11.6 23.6 %all-to-all-done = bf16[8,2,128,256]{3,2,1,0:T(8,128)(2,1)S(1)} async-done(((bf16[8,2,128,256]{3,2,1,0:T(8,128)(2,1)}), bf16[8,2,128,256]{3,2,1,0:T(8,128)(2,1)S(1)}, u32[]{:S(2)}, u32[]{:S(2)}) %all-to-all-start) | async-done | bytes 1048608 | tf_op jit(solution)/shard_map/all_to_all | solution.py:120
  35.3 0.0 copy-done
  35.3 70.9 %shard_map.64 = bf16[3,1024,128]{2,1,0:T(8,128)(2,1)S(1)} custom-call(s32[30]{0:T(128)S(1)} %reshape.65.source_ref, s32[3,10,128,128]{3,2,1,0:T(8,128)S(1)} %bitcast.36, bf16[16,128,256]{2,1,0:T(8,128)(2,1)S(1)} %bitcast.35, f32[3,32,256]{2,1,0:T(8,128)S(1)} %bitcast.37), custom_call_target="tpu_custom_call" | custom-call | tf_op jit(solution)/shard_map/pallas_call | solution.py:131
  106.2 0.1 fusion.1
  106.3 1.0 pad_maximum_fusion
  107.3 0.0 copy-start.1
  107.3 0.0 copy-start.2
  107.3 5.7 %all-to-all-start.1 = ((bf16[4,3,288,128]{3,2,1,0:T(8,128)(2,1)}), bf16[4,3,288,128]{3,2,1,0:T(8,128)(2,1)S(1)}, u32[]{:S(2)}, u32[]{:S(2)}) async-start(bf16[4,3,288,128]{3,2,1,0:T(8,128)(2,1)} %pad_maximum_fusion), calls=%async_computation.1 | async-start | bytes 1769472 | tf_op jit(solution)/shard_map/all_to_all | solution.py:162
  113.0 0.0 copy-done.1
  113.0 0.1 copy.22
  113.2 0.0 copy-done.2
  113.2 0.5 fusion
  113.7 1.7 %copy.24 = bf16[3,8,8,4,3,2,8]{6,5,4,3,2,1,0:T(2,128)(2,1)S(1)} copy(bf16[3,8,8,4,3,2,8]{1,2,6,0,4,5,3:T(8,128)(2,1)S(1)} %fusion) | data formatting | bytes 147456 | tf_op jit(solution)/shard_map/convert_element_type | solution.py:176
  115.4 0.7 reshape.71.band_ref
  116.1 8.8 %all-to-all-done.1.slab_ref = bf16[4,3,288,128]{3,2,1,0:T(8,128)(2,1)S(1)} async-done(((bf16[4,3,288,128]{3,2,1,0:T(8,128)(2,1)}), bf16[4,3,288,128]{3,2,1,0:T(8,128)(2,1)S(1)}, u32[]{:S(2)}, u32[]{:S(2)}) %all-to-all-start.1) | async-done | bytes 884768 | tf_op jit(solution)/shard_map/all_to_all | solution.py:162
  124.9 2.5 %shard_map.65 = bf16[3,8,16,8,128]{4,3,2,1,0:T(8,128)(2,1)} custom-call(bf16[4,3,288,128]{3,2,1,0:T(8,128)(2,1)S(1)} %all-to-all-done.1.slab_ref, bf16[192,192]{1,0:T(8,128)(2,1)S(1)} %reshape.71.band_ref), custom_call_target="tpu_custom_call" | custom-call | tf_op jit(solution)/shard_map/pallas_call | solution.py:179
  (5 shorter events, 0.1 us)
Async XLA Ops:
  4.2 6.5 %copy-start.3 = (s32[3,10]{1,0:T(4,128)S(1)}, s32[3,10]{1,0:T(4,128)}, u32[]{:S(2)}) copy-start(s32[3,10]{1,0:T(4,128)} %param.7) | copy-start | bytes 364
  4.2 31.1 %copy-start = (s32[3,10,64,2,128]{4,3,2,1,0:T(2,128)S(1)}, s32[3,10,64,2,128]{4,3,2,1,0:T(2,128)}, u32[]{:S(2)}) copy-start(s32[3,10,64,2,128]{4,3,2,1,0:T(2,128)} %param.9) | copy-start | bytes 5898244
  4.2 31.1 %all-to-all-start = ((bf16[8,2,128,256]{3,2,1,0:T(8,128)(2,1)}), bf16[8,2,128,256]{3,2,1,0:T(8,128)(2,1)S(1)}, u32[]{:S(2)}, u32[]{:S(2)}) async-start(bf16[8,2,128,256]{3,2,1,0:T(8,128)(2,1)} %broadcast_select_fusion), calls=%async_computation | async-start | bytes 2097152 | tf_op jit(solution)/shard_map/all_to_all | solution.py:120
  107.3 5.7 %copy-start.1 = (bf16[27,8,8]{0,2,1:T(8,128)(2,1)S(1)}, bf16[27,8,8]{0,2,1:T(8,128)(2,1)}, u32[]{:S(2)}) copy-start(bf16[27,8,8]{0,2,1:T(8,128)(2,1)} %param.10) | copy-start | bytes 10372
  107.3 5.8 %copy-start.2 = (bf16[8,4,2,3,1,1,1]{0,3,6,5,4,2,1:T(4,128)(2,1)S(1)}, bf16[8,4,2,3,1,1,1]{0,3,6,5,4,2,1:T(4,128)(2,1)}, u32[]{:S(2)}) copy-start(bf16[8,4,2,3,1,1,1]{0,3,6,5,4,2,1:T(4,128)(2,1)} %constant.42) | copy-start | bytes 1156
  107.3 17.5 %all-to-all-start.1 = ((bf16[4,3,288,128]{3,2,1,0:T(8,128)(2,1)}), bf16[4,3,288,128]{3,2,1,0:T(8,128)(2,1)S(1)}, u32[]{:S(2)}, u32[]{:S(2)}) async-start(bf16[4,3,288,128]{3,2,1,0:T(8,128)(2,1)} %pad_maximum_fusion), calls=%async_computation.1 | async-start | bytes 1769472 | tf_op jit(solution)/shard_map/all_to_all | solution.py:162

commit v2 on v1

--- a/solution.py
+++ b/solution.py
@@ -11,33 +11,141 @@
 LOW = 256
 
 
-def cost_kernel(sources, high, kinds, groups, source_ref, idx_ref, pool_ref, own_ref, out_ref):
+def fetch_kernel(
+    asked, ask_ref, tiles_ref, order_ref, pool_ref, stage, send_v, recv_v, send_x, recv_x, send_c, recv_c
+):
+    views = lax.axis_size("view")
+    shares = lax.axis_size("depth")
+    lines = shares // 2
+    view = lax.axis_index("view")
+    depth = lax.axis_index("depth")
+    line, core = depth // 2, depth % 2
+    other = line * 2 + 1 - core
+    width = stage.shape[-1]
+
+    def at_view(step):
+        return lax.rem(view + step + views, views)
+
+    def at_line(step):
+        return lax.rem(line + step + lines, lines) * 2 + core
+
+    def slots(owner):
+        return pl.ds(owner * asked, asked)
+
+    def copy(src, dst, send, recv, where):
+        return pltpu.make_async_remote_copy(
+            src_ref=src,
+            dst_ref=dst,
+            send_sem=send,
+            recv_sem=recv,
+            device_id=where,
+            device_id_type=pl.DeviceIdType.MESH,
+        )
+
+    barrier = pltpu.get_barrier_semaphore()
+    peers = [(at_view(o), depth) for o in range(1, views)]
+    peers += [(view, at_line(o)) for o in range(1, lines)]
+    peers += [(view, other)]
+    for peer in peers:
+        pl.semaphore_signal(barrier, inc=1, device_id=peer, device_id_type=pl.DeviceIdType.MESH)
+
+    start = pl.multiple_of(depth * width, width)
+    for owner in range(views):
+        for c in range(asked):
+            tile = tiles_ref[ask_ref[(owner * views + view) * asked + c], :, pl.ds(start, width)]
+            moved = jnp.dot(order_ref[...], tile, preferred_element_type=jnp.float32)
+            stage[owner, c] = moved.astype(jnp.bfloat16)
+    pl.semaphore_wait(barrier, len(peers))
+
+    over_view = []
+    for o in range(1, views):
+        step = copy(
+            stage.at[at_view(o)],
+            pool_ref.at[depth, slots(view)],
+            send_v.at[o - 1],
+            recv_v.at[o - 1],
+            (at_view(o), depth),
+        )
+        step.start()
+        over_view.append(step)
+    pool_ref[depth, slots(view)] = stage[view]
+
+    over_line, over_core = [], []
+    for o in range(views):
+        mine = pool_ref.at[depth, slots(at_view(-o))]
+        if o > 0:
+            copy(
+                stage.at[at_view(o)], mine, send_v.at[o - 1], recv_v.at[o - 1], (at_view(o), depth)
+            ).wait_recv()
+        for x in range(1, lines):
+            step = copy(
+                mine, mine, send_x.at[x - 1, o], recv_x.at[x - 1, o], (view, at_line(x))
+            )
+            step.start()
+            over_line.append(step)
+        step = copy(mine, mine, send_c.at[0, o], recv_c.at[0, o], (view, other))
+        step.start()
+        over_core.append(step)
+    for o in range(views):
+        for x in range(1, lines):
+            theirs = pool_ref.at[at_line(-x), slots(at_view(-o))]
+            copy(
+                theirs, theirs, send_x.at[x - 1, o], recv_x.at[x - 1, o], (view, at_line(x))
+            ).wait_recv()
+            step = copy(theirs, theirs, send_c.at[x, o], recv_c.at[x, o], (view, other))
+            step.start()
+            over_core.append(step)
+    for o in range(views):
+        for x in range(lines):
+            share = lax.rem(line - x + lines, lines) * 2 + 1 - core
+            there = pool_ref.at[share, slots(at_view(-o))]
+            copy(there, there, send_c.at[x, o], recv_c.at[x, o], (view, other)).wait_recv()
+    for step in over_view + over_line + over_core:
+        step.wait_send()
+
+
+def cost_kernel(
+    sources, high, kinds, groups, source_ref, idx_ref, pool_ref, own_ref, out_ref, low_ref, scale_ref
+):
     view = pl.program_id(0)
     columns = idx_ref.shape[-1]
     pairs = idx_ref.shape[2] // 2
     chans = kinds * groups
+    per = pool_ref.shape[0] // high
     iota = lax.broadcasted_iota(jnp.int32, (16, columns), 0).astype(jnp.float32)
     one = jnp.ones((16, columns), jnp.bfloat16)
     zero = jnp.zeros((16, columns), jnp.bfloat16)
     steps = [(iota + float(16 * m)).astype(jnp.bfloat16) for m in range(LOW // 16)]
 
+    live = jnp.zeros(scale_ref.shape, jnp.float32)
+    for k in range(sources):
+        usable = idx_ref[0, k] >= 0
+        low_ref[k] = jnp.where(usable, idx_ref[0, k] & (LOW - 1), -1).astype(jnp.float32)
+        live = live + jnp.where(usable, 1.0, 0.0)
+    scale_ref[...] = 0.5 / jnp.maximum(live, 1.0)
+
     def one_pair(pair, carry):
-        total = [jnp.zeros((groups, columns), jnp.float32) for _ in range(2)]
-        live = [jnp.zeros((groups, columns), jnp.float32) for _ in range(2)]
+        total = [[None] * kinds for _ in range(2)]
         for k in range(sources):
             hots, highs = [], []
             for q in range(2):
                 row = idx_ref[0, k, pl.ds(2 * pair + q, 1), :]
-                row = jnp.broadcast_to(row, (groups, columns))
-                usable = row >= 0
-                live[q] = live[q] + jnp.where(usable, 1.0, 0.0)
-                low = jnp.where(usable, row & (LOW - 1), -1).astype(jnp.float32)
-                low = jnp.concatenate([low, low], axis=0).astype(jnp.bfloat16)
+                highs.append(jnp.broadcast_to(row, (groups, columns)))
+                low = low_ref[k, pl.ds(2 * pair + q, 1), :]
+                low = jnp.broadcast_to(low, (16, columns)).astype(jnp.bfloat16)
                 hots.append(
                     jnp.concatenate([jnp.where(s == low, one, zero) for s in steps], axis=0)
                 )
-                highs.append(row)
-            table = pool_ref[source_ref[view * sources + k]]
+            source = source_ref[view * sources + k]
+            table = jnp.concatenate(
+                [
+                    jnp.concatenate(
+                        [pool_ref[h * per + i, source] for i in range(per)], axis=1
+                    )
+                    for h in range(high)
+                ],
+                axis=0,
+            )
             found = jnp.dot(
                 table, jnp.concatenate(hots, axis=1), preferred_element_type=jnp.float32
             )
@@ -60,9 +168,15 @@
                             jnp.where(bit, parts[2 * i + 1], parts[2 * i])
                             for i in range(len(parts) // 2)
                         ]
-                    own = own_ref[0, t * groups : (t + 1) * groups, q * columns : (q + 1) * columns]
-                    total[q] = total[q] + parts[0] * own
-        cost = [0.5 * total[q] / jnp.maximum(live[q], 1.0) for q in range(2)]
+                    total[q][t] = parts[0] if k == 0 else total[q][t] + parts[0]
+        cost = []
+        for q in range(2):
+            summed = None
+            for t in range(kinds):
+                own = own_ref[0, t * groups : (t + 1) * groups, q * columns : (q + 1) * columns]
+                term = total[q][t] * own
+                summed = term if summed is None else summed + term
+            cost.append(summed * scale_ref[pl.ds(2 * pair + q, 1), :])
         start = pl.multiple_of(pair * 2 * groups, 2 * groups)
         out_ref[0, pl.ds(start, 2 * groups), :] = jnp.concatenate(cost, axis=0).astype(jnp.bfloat16)
         return carry
@@ -101,7 +215,6 @@
 
 
 def on_device(features, view_lists, requests, warp_idx, conv_weight):
-    view_here = lax.axis_index("view")
     depth_here = lax.axis_index("depth")
     view_count = lax.axis_size("view")
     depth_count = lax.axis_size("depth")
@@ -113,12 +226,35 @@
     asked = requests.shape[2]
     rows = row_count * depth_count
 
-    tables = features.reshape(views, high, LOW, groups, kinds).transpose(0, 1, 4, 3, 2)
-    tables = tables.reshape(views, high * channels, LOW)
-    wanted = requests[:, view_here, :].reshape(-1)
-    outgoing = jnp.take(tables, wanted, axis=0).reshape(view_count, asked, high * channels, LOW)
-    pool = lax.all_to_all(outgoing, "view", split_axis=0, concat_axis=0, tiled=True)
-    pool = pool.reshape(view_count * asked, high * channels, LOW)
+    lines = depth_count // 2
+    share = pixels // depth_count
+    order = np.zeros((channels, channels), np.float32)
+    for c in range(channels):
+        order[(c % kinds) * groups + c // kinds, c] = 1.0
+    pool = pl.pallas_call(
+        functools.partial(fetch_kernel, asked),
+        out_shape=jax.ShapeDtypeStruct(
+            (depth_count, view_count * asked, channels, share), jnp.bfloat16
+        ),
+        in_specs=[
+            pl.BlockSpec(memory_space=pltpu.SMEM),
+            pl.BlockSpec(memory_space=pltpu.VMEM),
+            pl.BlockSpec(memory_space=pltpu.VMEM),
+        ],
+        out_specs=pl.BlockSpec(memory_space=pltpu.VMEM),
+        scratch_shapes=[
+            pltpu.VMEM((view_count, asked, channels, share), jnp.bfloat16),
+            pltpu.SemaphoreType.DMA((view_count - 1,)),
+            pltpu.SemaphoreType.DMA((view_count - 1,)),
+            pltpu.SemaphoreType.DMA((lines, view_count)),
+            pltpu.SemaphoreType.DMA((lines, view_count)),
+            pltpu.SemaphoreType.DMA((lines, view_count)),
+            pltpu.SemaphoreType.DMA((lines, view_count)),
+        ],
+        compiler_params=pltpu.CompilerParams(
+            collective_id=0, has_side_effects=True, vmem_limit_bytes=16 * 1024 * 1024
+        ),
+    )(requests.reshape(-1), features.transpose(0, 2, 1), jnp.asarray(order, jnp.bfloat16))
 
     own_pixels = row_count * columns
     own = lax.dynamic_slice_in_dim(features, depth_here * own_pixels, own_pixels, 1)
@@ -135,12 +271,16 @@
             grid=(views,),
             in_specs=[
                 pl.BlockSpec((1, sources, planes * row_count, columns), lambda v, s: (v, 0, 0, 0)),
-                pl.BlockSpec(pool.shape, lambda v, s: (0, 0, 0)),
+                pl.BlockSpec(pool.shape, lambda v, s: (0, 0, 0, 0)),
                 pl.BlockSpec((1,) + own.shape[1:], lambda v, s: (v, 0, 0)),
             ],
             out_specs=pl.BlockSpec(
                 (1, planes * row_count * groups, columns), lambda v, s: (v, 0, 0)
             ),
+            scratch_shapes=[
+                pltpu.VMEM((sources, planes * row_count, columns), jnp.float32),
+                pltpu.VMEM((planes * row_count, columns), jnp.float32),
+            ],
         ),
         out_shape=jax.ShapeDtypeStruct(
             (views, planes * row_count * groups, columns), jnp.bfloat16

time: 129 us -> 114 us (0.88)
  waiting for transfers between devices: 32.4 us -> 8.76 us
  Pallas kernels: 73.4 us -> 90.7 us
  starting transfers between devices: 12.2 us -> 3.72 us
  local copies, waits for them, and re-layouts: 5.73 us -> 7.52 us
    all_to_all x1 -> x0, waiting for transfers between devices: 23.6 us -> none  [on_device(): lax.all_to_all(outgoing, 'view', split_axis=0, concat_axis=0, tiled=True)]
    pallas_call x0 -> x1, Pallas kernels: none -> 17.9 us  [on_device(): pl.pallas_call(functools.partial(fetch_kernel, asked), out_shape=jax.Shap...]
    all_to_all x1 -> x0, starting transfers between devices: 6.51 us -> none  [on_device(): lax.all_to_all(outgoing, 'view', split_axis=0, concat_axis=0, tiled=True)]
    unnamed x9 -> x12, local copies, waits for them, and re-layouts: 0.16 us -> 4.12 us
    all_to_all x1, starting transfers between devices: 5.7 us -> 3.72 us  [on_device(): lax.all_to_all(slabs, 'depth', split_axis=0, concat_axis=0, tiled=True)]
  transfers between devices with their start and end apart: 2 -> 1, of which waited for: 2 -> 1; matrix products, arithmetic and copies ran while one was open for 3% -> 3% of each run, Pallas kernels for 0% -> 0%
where the time goes in v2:
time: 114 us; the launch traced here: 113 us
  Pallas kernels  90.7 us (80%)
  waiting for transfers between devices  8.76 us (8%)
  local copies, waits for them, and re-layouts  7.52 us (7%)
  starting transfers between devices  3.72 us (3%)
  other arithmetic  1.86 us (2%)
    pallas_call x1, Pallas kernels, on_device(): pl.pallas_call(functools.partial(cost_kernel, sources, high, kinds, group...  70.3 us
    pallas_call x1, Pallas kernels, on_device(): pl.pallas_call(functools.partial(fetch_kernel, asked), out_shape=jax.Shap...  17.9 us
    all_to_all x1, waiting for transfers between devices, on_device(): lax.all_to_all(slabs, 'depth', split_axis=0, concat_axis=0, tiled=True)  8.76 us
    unnamed x12, local copies, waits for them, and re-layouts  4.12 us
    all_to_all x1, starting transfers between devices, on_device(): lax.all_to_all(slabs, 'depth', split_axis=0, concat_axis=0, tiled=True)  3.72 us
    pallas_call x1, Pallas kernels, on_device(): pl.pallas_call(functools.partial(conv_kernel, slab_planes, groups, rows),...  2.47 us
  transfers between devices with their start and end apart: 1, of which 1 were waited for; matrix products, arithmetic and copies ran while one was open for 3% of the time, Pallas kernels for 0%

profile of v2, /device:TPU:1, one launch (start us, length us, event | category | flops | bytes accessed | tf_op | source)
XLA Modules:
  0.0 113.2 jit_solution(6763019959648955418)
XLA Ops:
  0.0 0.8 reshape.21.source_ref
  0.8 0.8 copy.12
  1.6 0.1 reshape.23.ask_ref
  1.7 0.8 dynamic-slice_convert_fusion
  2.6 0.0 copy-start.1
  2.6 0.9 copy-done.1
  3.5 0.0 copy-start.2
  3.5 0.7 copy-done.2
  4.2 17.9 %shard_map.73.pool_ref = bf16[4,16,32,256]{3,2,1,0:T(8,128)(2,1)S(1)} custom-call(s32[128]{0:T(128)S(1)} %reshape.23.ask_ref, bf16[3,32,1024]{2,1,0:T(8,128)(2,1)S(1)} %bitcast.28, bf16[32,32]{1,0:T(8,128)(2,1)S(1)} %copy-done.2), custom_call_target="tpu_custom_call" | custom-call | tf_op jit(solution)/shard_map/pallas_call | solution.py:234
  22.1 0.0 copy-start
  22.2 1.5 %copy-done = s32[3,10,64,2,128]{4,3,2,1,0:T(2,128)S(1)} copy-done((s32[3,10,64,2,128]{4,3,2,1,0:T(2,128)S(1)}, s32[3,10,64,2,128]{4,3,2,1,0:T(2,128)}, u32[]{:S(2)}) %copy-start) | copy-done | bytes 1966104
  23.7 70.3 %shard_map.74 = bf16[3,1024,128]{2,1,0:T(8,128)(2,1)S(1)} custom-call(s32[30]{0:T(128)S(1)} %reshape.21.source_ref, s32[3,10,128,128]{3,2,1,0:T(8,128)S(1)} %bitcast.26, bf16[4,16,32,256]{3,2,1,0:T(8,128)(2,1)S(1)} %shard_map.73.pool_ref, f32[3,32,256]{2,1,0:T(8,128)S(1)} %bitcast.27), custom_call_target="tpu_custom_call" | custom-call | tf_op jit(solution)/shard_map/pallas_call | solution.py:267
  94.0 0.1 fusion.1
  94.1 1.0 pad_maximum_fusion
  95.2 0.0 copy-start.3
  95.2 0.0 copy-start.4
  95.2 3.7 %all-to-all-start = ((bf16[4,3,288,128]{3,2,1,0:T(8,128)(2,1)}), bf16[4,3,288,128]{3,2,1,0:T(8,128)(2,1)S(1)}, u32[]{:S(2)}, u32[]{:S(2)}) async-start(bf16[4,3,288,128]{3,2,1,0:T(8,128)(2,1)} %pad_maximum_fusion), calls=%async_computation | async-start | bytes 1769472 | tf_op jit(solution)/shard_map/all_to_all | solution.py:302
  98.9 0.0 copy-done.3
  98.9 0.1 copy.14
  99.0 0.0 copy-done.4
  99.0 0.5 fusion
  99.5 1.7 %copy.16 = bf16[3,8,8,4,3,2,8]{6,5,4,3,2,1,0:T(2,128)(2,1)S(1)} copy(bf16[3,8,8,4,3,2,8]{1,2,6,0,4,5,3:T(8,128)(2,1)S(1)} %fusion) | data formatting | bytes 147456 | tf_op jit(solution)/shard_map/convert_element_type | solution.py:316
  101.2 0.7 reshape.25.band_ref
  102.0 8.8 %all-to-all-done.slab_ref = bf16[4,3,288,128]{3,2,1,0:T(8,128)(2,1)S(1)} async-done(((bf16[4,3,288,128]{3,2,1,0:T(8,128)(2,1)}), bf16[4,3,288,128]{3,2,1,0:T(8,128)(2,1)S(1)}, u32[]{:S(2)}, u32[]{:S(2)}) %all-to-all-start) | async-done | bytes 884768 | tf_op jit(solution)/shard_map/all_to_all | solution.py:302
  110.7 2.5 %shard_map.75 = bf16[3,8,16,8,128]{4,3,2,1,0:T(8,128)(2,1)} custom-call(bf16[4,3,288,128]{3,2,1,0:T(8,128)(2,1)S(1)} %all-to-all-done.slab_ref, bf16[192,192]{1,0:T(8,128)(2,1)S(1)} %reshape.25.band_ref), custom_call_target="tpu_custom_call" | custom-call | tf_op jit(solution)/shard_map/pallas_call | solution.py:319
  (2 shorter events, 0.0 us)
Async XLA Ops:
  2.6 0.9 copy-start.1
  3.5 0.7 copy-start.2
  22.1 1.5 %copy-start = (s32[3,10,64,2,128]{4,3,2,1,0:T(2,128)S(1)}, s32[3,10,64,2,128]{4,3,2,1,0:T(2,128)}, u32[]{:S(2)}) copy-start(s32[3,10,64,2,128]{4,3,2,1,0:T(2,128)} %param.10) | copy-start | bytes 5898244
  95.2 3.7 %copy-start.3 = (bf16[27,8,8]{0,2,1:T(8,128)(2,1)S(1)}, bf16[27,8,8]{0,2,1:T(8,128)(2,1)}, u32[]{:S(2)}) copy-start(bf16[27,8,8]{0,2,1:T(8,128)(2,1)} %param.11) | copy-start | bytes 10372
  95.2 3.9 %copy-start.4 = (bf16[8,4,2,3,1,1,1]{0,3,6,5,4,2,1:T(4,128)(2,1)S(1)}, bf16[8,4,2,3,1,1,1]{0,3,6,5,4,2,1:T(4,128)(2,1)}, u32[]{:S(2)}) copy-start(bf16[8,4,2,3,1,1,1]{0,3,6,5,4,2,1:T(4,128)(2,1)} %constant.23) | copy-start | bytes 1156
  95.2 15.6 %all-to-all-start = ((bf16[4,3,288,128]{3,2,1,0:T(8,128)(2,1)}), bf16[4,3,288,128]{3,2,1,0:T(8,128)(2,1)S(1)}, u32[]{:S(2)}, u32[]{:S(2)}) async-start(bf16[4,3,288,128]{3,2,1,0:T(8,128)(2,1)} %pad_maximum_fusion), calls=%async_computation | async-start | bytes 1769472 | tf_op jit(solution)/shard_map/all_to_all | solution.py:302

commit v3 on v2

--- a/solution.py
+++ b/solution.py
@@ -8,7 +8,7 @@
 from jax.experimental.pallas import tpu as pltpu
 from jax.sharding import PartitionSpec as P
 
-LOW = 256
+LOW = 128
 
 
 def fetch_kernel(
@@ -111,7 +111,7 @@
     columns = idx_ref.shape[-1]
     pairs = idx_ref.shape[2] // 2
     chans = kinds * groups
-    per = pool_ref.shape[0] // high
+    share = pool_ref.shape[-1]
     iota = lax.broadcasted_iota(jnp.int32, (16, columns), 0).astype(jnp.float32)
     one = jnp.ones((16, columns), jnp.bfloat16)
     zero = jnp.zeros((16, columns), jnp.bfloat16)
@@ -139,9 +139,7 @@
             source = source_ref[view * sources + k]
             table = jnp.concatenate(
                 [
-                    jnp.concatenate(
-                        [pool_ref[h * per + i, source] for i in range(per)], axis=1
-                    )
+                    pool_ref[h * LOW // share, source, :, h * LOW % share : h * LOW % share + LOW]
                     for h in range(high)
                 ],
                 axis=0,

time: 114 us -> 144 us (1.26)
  Pallas kernels: 90.7 us -> 120 us
    pallas_call x1, Pallas kernels: 70.3 us -> 99.9 us  [on_device(): pl.pallas_call(functools.partial(cost_kernel, sources, high, kinds, group...]
  transfers between devices with their start and end apart: 1 -> 1, of which waited for: 1 -> 1; matrix products, arithmetic and copies ran while one was open for 3% -> 2% of each run, Pallas kernels for 0% -> 0%
where the time goes in v3:
time: 144 us; the launch traced here: 143 us
  Pallas kernels  120 us (83%)
  waiting for transfers between devices  8.76 us (6%)
  local copies, waits for them, and re-layouts  7.52 us (5%)
  starting transfers between devices  3.72 us (3%)
  other arithmetic  1.86 us (1%)
    pallas_call x1, Pallas kernels, on_device(): pl.pallas_call(functools.partial(cost_kernel, sources, high, kinds, group...  99.9 us
    pallas_call x1, Pallas kernels, on_device(): pl.pallas_call(functools.partial(fetch_kernel, asked), out_shape=jax.Shap...  17.9 us
    all_to_all x1, waiting for transfers between devices, on_device(): lax.all_to_all(slabs, 'depth', split_axis=0, concat_axis=0, tiled=True)  8.76 us
    unnamed x12, local copies, waits for them, and re-layouts  4.12 us
    all_to_all x1, starting transfers between devices, on_device(): lax.all_to_all(slabs, 'depth', split_axis=0, concat_axis=0, tiled=True)  3.72 us
  transfers between devices with their start and end apart: 1, of which 1 were waited for; matrix products, arithmetic and copies ran while one was open for 2% of the time, Pallas kernels for 0%

profile of v3, /device:TPU:1, one launch (start us, length us, event | category | flops | bytes accessed | tf_op | source)
XLA Modules:
  0.0 142.7 jit_solution(3807723138538265842)
XLA Ops:
  0.0 0.8 reshape.21.source_ref
  0.8 0.8 copy.12
  1.6 0.1 reshape.23.ask_ref
  1.7 0.8 dynamic-slice_convert_fusion
  2.6 0.0 copy-start.1
  2.6 0.9 copy-done.1
  3.5 0.0 copy-start.2
  3.5 0.7 copy-done.2
  4.2 17.9 %shard_map.73.pool_ref = bf16[4,16,32,256]{3,2,1,0:T(8,128)(2,1)S(1)} custom-call(s32[128]{0:T(128)S(1)} %reshape.23.ask_ref, bf16[3,32,1024]{2,1,0:T(8,128)(2,1)S(1)} %bitcast.28, bf16[32,32]{1,0:T(8,128)(2,1)S(1)} %copy-done.2), custom_call_target="tpu_custom_call" | custom-call | tf_op jit(solution)/shard_map/pallas_call | solution.py:232
  22.1 0.0 copy-start
  22.2 1.5 %copy-done = s32[3,10,64,2,128]{4,3,2,1,0:T(2,128)S(1)} copy-done((s32[3,10,64,2,128]{4,3,2,1,0:T(2,128)S(1)}, s32[3,10,64,2,128]{4,3,2,1,0:T(2,128)}, u32[]{:S(2)}) %copy-start) | copy-done | bytes 1966104
  23.7 99.9 %shard_map.74 = bf16[3,1024,128]{2,1,0:T(8,128)(2,1)S(1)} custom-call(s32[30]{0:T(128)S(1)} %reshape.21.source_ref, s32[3,10,128,128]{3,2,1,0:T(8,128)S(1)} %bitcast.26, bf16[4,16,32,256]{3,2,1,0:T(8,128)(2,1)S(1)} %shard_map.73.pool_ref, f32[3,32,256]{2,1,0:T(8,128)S(1)} %bitcast.27), custom_call_target="tpu_custom_call" | custom-call | tf_op jit(solution)/shard_map/pallas_call | solution.py:265
  123.6 0.1 fusion.1
  123.7 1.0 pad_maximum_fusion
  124.7 0.0 copy-start.3
  124.7 0.0 copy-start.4
  124.7 3.7 %all-to-all-start = ((bf16[4,3,288,128]{3,2,1,0:T(8,128)(2,1)}), bf16[4,3,288,128]{3,2,1,0:T(8,128)(2,1)S(1)}, u32[]{:S(2)}, u32[]{:S(2)}) async-start(bf16[4,3,288,128]{3,2,1,0:T(8,128)(2,1)} %pad_maximum_fusion), calls=%async_computation | async-start | bytes 1769472 | tf_op jit(solution)/shard_map/all_to_all | solution.py:300
  128.4 0.0 copy-done.3
  128.4 0.1 copy.14
  128.6 0.0 copy-done.4
  128.6 0.5 fusion
  129.1 1.7 %copy.16 = bf16[3,8,8,4,3,2,8]{6,5,4,3,2,1,0:T(2,128)(2,1)S(1)} copy(bf16[3,8,8,4,3,2,8]{1,2,6,0,4,5,3:T(8,128)(2,1)S(1)} %fusion) | data formatting | bytes 147456 | tf_op jit(solution)/shard_map/convert_element_type | solution.py:314
  130.8 0.7 reshape.25.band_ref
  131.5 8.8 %all-to-all-done.slab_ref = bf16[4,3,288,128]{3,2,1,0:T(8,128)(2,1)S(1)} async-done(((bf16[4,3,288,128]{3,2,1,0:T(8,128)(2,1)}), bf16[4,3,288,128]{3,2,1,0:T(8,128)(2,1)S(1)}, u32[]{:S(2)}, u32[]{:S(2)}) %all-to-all-start) | async-done | bytes 884768 | tf_op jit(solution)/shard_map/all_to_all | solution.py:300
  140.3 2.5 %shard_map.75 = bf16[3,8,16,8,128]{4,3,2,1,0:T(8,128)(2,1)} custom-call(bf16[4,3,288,128]{3,2,1,0:T(8,128)(2,1)S(1)} %all-to-all-done.slab_ref, bf16[192,192]{1,0:T(8,128)(2,1)S(1)} %reshape.25.band_ref), custom_call_target="tpu_custom_call" | custom-call | tf_op jit(solution)/shard_map/pallas_call | solution.py:317
  (2 shorter events, 0.0 us)
Async XLA Ops:
  2.6 0.9 copy-start.1
  3.5 0.7 copy-start.2
  22.1 1.5 %copy-start = (s32[3,10,64,2,128]{4,3,2,1,0:T(2,128)S(1)}, s32[3,10,64,2,128]{4,3,2,1,0:T(2,128)}, u32[]{:S(2)}) copy-start(s32[3,10,64,2,128]{4,3,2,1,0:T(2,128)} %param.10) | copy-start | bytes 5898244
  124.7 3.7 %copy-start.3 = (bf16[27,8,8]{0,2,1:T(8,128)(2,1)S(1)}, bf16[27,8,8]{0,2,1:T(8,128)(2,1)}, u32[]{:S(2)}) copy-start(bf16[27,8,8]{0,2,1:T(8,128)(2,1)} %param.11) | copy-start | bytes 10372
  124.7 3.9 %copy-start.4 = (bf16[8,4,2,3,1,1,1]{0,3,6,5,4,2,1:T(4,128)(2,1)S(1)}, bf16[8,4,2,3,1,1,1]{0,3,6,5,4,2,1:T(4,128)(2,1)}, u32[]{:S(2)}) copy-start(bf16[8,4,2,3,1,1,1]{0,3,6,5,4,2,1:T(4,128)(2,1)} %constant.23) | copy-start | bytes 1156
  124.7 15.6 %all-to-all-start = ((bf16[4,3,288,128]{3,2,1,0:T(8,128)(2,1)}), bf16[4,3,288,128]{3,2,1,0:T(8,128)(2,1)S(1)}, u32[]{:S(2)}, u32[]{:S(2)}) async-start(bf16[4,3,288,128]{3,2,1,0:T(8,128)(2,1)} %pad_maximum_fusion), calls=%async_computation | async-start | bytes 1769472 | tf_op jit(solution)/shard_map/all_to_all | solution.py:300

commit v4 on v2

--- a/solution.py
+++ b/solution.py
@@ -105,17 +105,33 @@
 
 
 def cost_kernel(
-    sources, high, kinds, groups, source_ref, idx_ref, pool_ref, own_ref, out_ref, low_ref, scale_ref
+    sources, high, kinds, groups, source_ref, idx_ref, pool_ref, own_ref, out_ref, table_ref, low_ref, scale_ref
 ):
     view = pl.program_id(0)
     columns = idx_ref.shape[-1]
     pairs = idx_ref.shape[2] // 2
-    chans = kinds * groups
     per = pool_ref.shape[0] // high
     iota = lax.broadcasted_iota(jnp.int32, (16, columns), 0).astype(jnp.float32)
     one = jnp.ones((16, columns), jnp.bfloat16)
     zero = jnp.zeros((16, columns), jnp.bfloat16)
     steps = [(iota + float(16 * m)).astype(jnp.bfloat16) for m in range(LOW // 16)]
+
+    @pl.when(view == 0)
+    def _():
+        for slot in range(pool_ref.shape[1]):
+            parts = [
+                jnp.concatenate([pool_ref[h * per + i, slot] for i in range(per)], axis=1)
+                for h in range(high)
+            ]
+            parts = [part.astype(jnp.float32) for part in parts]
+            table_ref[slot] = jnp.concatenate(
+                [
+                    parts[h][t * groups : (t + 1) * groups]
+                    for t in range(kinds)
+                    for h in range(high)
+                ],
+                axis=0,
+            ).astype(jnp.bfloat16)
 
     live = jnp.zeros(scale_ref.shape, jnp.float32)
     for k in range(sources):
@@ -136,16 +152,7 @@
                 hots.append(
                     jnp.concatenate([jnp.where(s == low, one, zero) for s in steps], axis=0)
                 )
-            source = source_ref[view * sources + k]
-            table = jnp.concatenate(
-                [
-                    jnp.concatenate(
-                        [pool_ref[h * per + i, source] for i in range(per)], axis=1
-                    )
-                    for h in range(high)
-                ],
-                axis=0,
-            )
+            table = table_ref[source_ref[view * sources + k]]
             found = jnp.dot(
                 table, jnp.concatenate(hots, axis=1), preferred_element_type=jnp.float32
             )
@@ -158,7 +165,7 @@
                 for t in range(kinds):
                     parts = [
                         found[
-                            h * chans + t * groups : h * chans + (t + 1) * groups,
+                            (t * high + h) * groups : (t * high + h + 1) * groups,
                             q * columns : (q + 1) * columns,
                         ]
                         for h in range(high)
@@ -278,6 +285,7 @@
                 (1, planes * row_count * groups, columns), lambda v, s: (v, 0, 0)
             ),
             scratch_shapes=[
+                pltpu.VMEM((view_count * asked, high * channels, LOW), jnp.bfloat16),
                 pltpu.VMEM((sources, planes * row_count, columns), jnp.float32),
                 pltpu.VMEM((planes * row_count, columns), jnp.float32),
             ],

time: 114 us -> 113 us (level)
  Pallas kernels: 90.7 us -> 89.4 us
    pallas_call x1, Pallas kernels: 70.3 us -> 69 us  [on_device(): pl.pallas_call(functools.partial(cost_kernel, sources, high, kinds, group...]
where the time goes in v4:
time: 113 us; the launch traced here: 112 us
  Pallas kernels  89.4 us (79%)
  waiting for transfers between devices  8.76 us (8%)
  local copies, waits for them, and re-layouts  7.52 us (7%)
  starting transfers between devices  3.71 us (3%)
  other arithmetic  1.86 us (2%)
    pallas_call x1, Pallas kernels, on_device(): pl.pallas_call(functools.partial(cost_kernel, sources, high, kinds, group...  69 us
    pallas_call x1, Pallas kernels, on_device(): pl.pallas_call(functools.partial(fetch_kernel, asked), out_shape=jax.Shap...  17.9 us
    all_to_all x1, waiting for transfers between devices, on_device(): lax.all_to_all(slabs, 'depth', split_axis=0, concat_axis=0, tiled=True)  8.76 us
    unnamed x12, local copies, waits for them, and re-layouts  4.12 us
    all_to_all x1, starting transfers between devices, on_device(): lax.all_to_all(slabs, 'depth', split_axis=0, concat_axis=0, tiled=True)  3.71 us
    pallas_call x1, Pallas kernels, on_device(): pl.pallas_call(functools.partial(conv_kernel, slab_planes, groups, rows),...  2.46 us
  transfers between devices with their start and end apart: 1, of which 1 were waited for; matrix products, arithmetic and copies ran while one was open for 3% of the time, Pallas kernels for 0%

profile of v4, /device:TPU:1, one launch (start us, length us, event | category | flops | bytes accessed | tf_op | source)
XLA Modules:
  0.0 111.8 jit_solution(16593251815298850347)
XLA Ops:
  0.0 0.8 reshape.21.source_ref
  0.8 0.8 copy.12
  1.6 0.1 reshape.23.ask_ref
  1.7 0.8 dynamic-slice_convert_fusion
  2.6 0.0 copy-start.1
  2.6 0.9 copy-done.1
  3.5 0.0 copy-start.2
  3.5 0.7 copy-done.2
  4.2 17.9 %shard_map.73.pool_ref = bf16[4,16,32,256]{3,2,1,0:T(8,128)(2,1)S(1)} custom-call(s32[128]{0:T(128)S(1)} %reshape.23.ask_ref, bf16[3,32,1024]{2,1,0:T(8,128)(2,1)S(1)} %bitcast.28, bf16[32,32]{1,0:T(8,128)(2,1)S(1)} %copy-done.2), custom_call_target="tpu_custom_call" | custom-call | tf_op jit(solution)/shard_map/pallas_call | solution.py:241
  22.1 0.0 copy-start
  22.2 1.5 %copy-done = s32[3,10,64,2,128]{4,3,2,1,0:T(2,128)S(1)} copy-done((s32[3,10,64,2,128]{4,3,2,1,0:T(2,128)S(1)}, s32[3,10,64,2,128]{4,3,2,1,0:T(2,128)}, u32[]{:S(2)}) %copy-start) | copy-done | bytes 1966104
  23.7 69.0 %shard_map.74 = bf16[3,1024,128]{2,1,0:T(8,128)(2,1)S(1)} custom-call(s32[30]{0:T(128)S(1)} %reshape.21.source_ref, s32[3,10,128,128]{3,2,1,0:T(8,128)S(1)} %bitcast.26, bf16[4,16,32,256]{3,2,1,0:T(8,128)(2,1)S(1)} %shard_map.73.pool_ref, f32[3,32,256]{2,1,0:T(8,128)S(1)} %bitcast.27), custom_call_target="tpu_custom_call" | custom-call | tf_op jit(solution)/shard_map/pallas_call | solution.py:274
  92.7 0.1 fusion.1
  92.8 1.0 pad_maximum_fusion
  93.8 0.0 copy-start.3
  93.8 0.0 copy-start.4
  93.8 3.7 %all-to-all-start = ((bf16[4,3,288,128]{3,2,1,0:T(8,128)(2,1)}), bf16[4,3,288,128]{3,2,1,0:T(8,128)(2,1)S(1)}, u32[]{:S(2)}, u32[]{:S(2)}) async-start(bf16[4,3,288,128]{3,2,1,0:T(8,128)(2,1)} %pad_maximum_fusion), calls=%async_computation | async-start | bytes 1769472 | tf_op jit(solution)/shard_map/all_to_all | solution.py:310
  97.5 0.0 copy-done.3
  97.5 0.1 copy.14
  97.7 0.0 copy-done.4
  97.7 0.5 fusion
  98.2 1.7 %copy.16 = bf16[3,8,8,4,3,2,8]{6,5,4,3,2,1,0:T(2,128)(2,1)S(1)} copy(bf16[3,8,8,4,3,2,8]{1,2,6,0,4,5,3:T(8,128)(2,1)S(1)} %fusion) | data formatting | bytes 147456 | tf_op jit(solution)/shard_map/convert_element_type | solution.py:324
  99.9 0.7 reshape.25.band_ref
  100.6 8.8 %all-to-all-done.slab_ref = bf16[4,3,288,128]{3,2,1,0:T(8,128)(2,1)S(1)} async-done(((bf16[4,3,288,128]{3,2,1,0:T(8,128)(2,1)}), bf16[4,3,288,128]{3,2,1,0:T(8,128)(2,1)S(1)}, u32[]{:S(2)}, u32[]{:S(2)}) %all-to-all-start) | async-done | bytes 884768 | tf_op jit(solution)/shard_map/all_to_all | solution.py:310
  109.4 2.5 %shard_map.75 = bf16[3,8,16,8,128]{4,3,2,1,0:T(8,128)(2,1)} custom-call(bf16[4,3,288,128]{3,2,1,0:T(8,128)(2,1)S(1)} %all-to-all-done.slab_ref, bf16[192,192]{1,0:T(8,128)(2,1)S(1)} %reshape.25.band_ref), custom_call_target="tpu_custom_call" | custom-call | tf_op jit(solution)/shard_map/pallas_call | solution.py:327
  (2 shorter events, 0.0 us)
Async XLA Ops:
  2.6 0.9 copy-start.1
  3.5 0.7 copy-start.2
  22.1 1.5 %copy-start = (s32[3,10,64,2,128]{4,3,2,1,0:T(2,128)S(1)}, s32[3,10,64,2,128]{4,3,2,1,0:T(2,128)}, u32[]{:S(2)}) copy-start(s32[3,10,64,2,128]{4,3,2,1,0:T(2,128)} %param.10) | copy-start | bytes 5898244
  93.8 3.7 %copy-start.3 = (bf16[27,8,8]{0,2,1:T(8,128)(2,1)S(1)}, bf16[27,8,8]{0,2,1:T(8,128)(2,1)}, u32[]{:S(2)}) copy-start(bf16[27,8,8]{0,2,1:T(8,128)(2,1)} %param.11) | copy-start | bytes 10372
  93.8 3.9 %copy-start.4 = (bf16[8,4,2,3,1,1,1]{0,3,6,5,4,2,1:T(4,128)(2,1)S(1)}, bf16[8,4,2,3,1,1,1]{0,3,6,5,4,2,1:T(4,128)(2,1)}, u32[]{:S(2)}) copy-start(bf16[8,4,2,3,1,1,1]{0,3,6,5,4,2,1:T(4,128)(2,1)} %constant.23) | copy-start | bytes 1156
  93.8 15.6 %all-to-all-start = ((bf16[4,3,288,128]{3,2,1,0:T(8,128)(2,1)}), bf16[4,3,288,128]{3,2,1,0:T(8,128)(2,1)S(1)}, u32[]{:S(2)}, u32[]{:S(2)}) async-start(bf16[4,3,288,128]{3,2,1,0:T(8,128)(2,1)} %pad_maximum_fusion), calls=%async_computation | async-start | bytes 1769472 | tf_op jit(solution)/shard_map/all_to_all | solution.py:310

commit v5 on v3

--- a/solution.py
+++ b/solution.py
@@ -8,7 +8,7 @@
 from jax.experimental.pallas import tpu as pltpu
 from jax.sharding import PartitionSpec as P
 
-LOW = 128
+LOW = 256
 
 
 def fetch_kernel(
@@ -105,97 +105,208 @@
 
 
 def cost_kernel(
-    sources, high, kinds, groups, source_ref, idx_ref, pool_ref, own_ref, out_ref, low_ref, scale_ref
+    kinds,
+    groups,
+    inner,
+    source_ref,
+    idx_ref,
+    pool_ref,
+    own_ref,
+    slabs_ref,
+    cost_ref,
+    table_ref,
+    low_ref,
+    scale_ref,
+    send_sem,
+    recv_sem,
 ):
-    view = pl.program_id(0)
-    columns = idx_ref.shape[-1]
-    pairs = idx_ref.shape[2] // 2
-    chans = kinds * groups
-    share = pool_ref.shape[-1]
-    iota = lax.broadcasted_iota(jnp.int32, (16, columns), 0).astype(jnp.float32)
-    one = jnp.ones((16, columns), jnp.bfloat16)
-    zero = jnp.zeros((16, columns), jnp.bfloat16)
-    steps = [(iota + float(16 * m)).astype(jnp.bfloat16) for m in range(LOW // 16)]
-
-    live = jnp.zeros(scale_ref.shape, jnp.float32)
-    for k in range(sources):
-        usable = idx_ref[0, k] >= 0
-        low_ref[k] = jnp.where(usable, idx_ref[0, k] & (LOW - 1), -1).astype(jnp.float32)
-        live = live + jnp.where(usable, 1.0, 0.0)
-    scale_ref[...] = 0.5 / jnp.maximum(live, 1.0)
-
-    def one_pair(pair, carry):
-        total = [[None] * kinds for _ in range(2)]
+    views, sources, lines, columns = idx_ref.shape
+    slots, chans, share = pool_ref.shape[1:]
+    high = table_ref.shape[1] // chans
+    per = LOW // share
+    shares = lax.axis_size("depth")
+    view_here = lax.axis_index("view")
+    depth = lax.axis_index("depth")
+    slab = slabs_ref.shape[2]
+    rim = (slab - inner) // 2
+
+    barrier = pltpu.get_barrier_semaphore()
+    for o in range(1, shares):
+        pl.semaphore_signal(
+            barrier,
+            inc=1,
+            device_id=(view_here, lax.rem(depth + o, shares)),
+            device_id_type=pl.DeviceIdType.MESH,
+        )
+
+    def one_table(slot, carry):
+        parts = [
+            jnp.concatenate([pool_ref[h * per + i, slot] for i in range(per)], axis=1)
+            for h in range(high)
+        ]
+        parts = [part.astype(jnp.float32) for part in parts]
+        table_ref[slot] = jnp.concatenate(
+            [parts[h][t * groups : (t + 1) * groups] for t in range(kinds) for h in range(high)],
+            axis=0,
+        ).astype(jnp.bfloat16)
+        return carry
+
+    lax.fori_loop(0, slots, one_table, 0)
+    empty = jnp.zeros((rim, columns), jnp.bfloat16)
+    for view in range(views):
+        cost_ref[view, :rim] = empty
+        cost_ref[view, rim + lines * groups :] = empty
+
+    count = lax.broadcasted_iota(jnp.int32, (LOW, columns), 0).astype(jnp.float32)
+    count = count.astype(jnp.bfloat16)
+    one = jnp.ones((LOW, columns), jnp.bfloat16)
+    zero = jnp.zeros((LOW, columns), jnp.bfloat16)
+
+    def slab_copy(o, view):
+        to = lax.rem(depth + o, shares)
+        start = pl.multiple_of(to * inner, inner)
+        return pltpu.make_async_remote_copy(
+            src_ref=cost_ref.at[view, pl.ds(start, slab)],
+            dst_ref=slabs_ref.at[depth, view],
+            send_sem=send_sem.at[o - 1, view],
+            recv_sem=recv_sem.at[o - 1, view],
+            device_id=(view_here, to),
+            device_id_type=pl.DeviceIdType.MESH,
+        )
+
+    def one_view(view, carry):
+        live = jnp.zeros(scale_ref.shape, jnp.float32)
         for k in range(sources):
-            hots, highs = [], []
-            for q in range(2):
-                row = idx_ref[0, k, pl.ds(2 * pair + q, 1), :]
-                highs.append(jnp.broadcast_to(row, (groups, columns)))
-                low = low_ref[k, pl.ds(2 * pair + q, 1), :]
-                low = jnp.broadcast_to(low, (16, columns)).astype(jnp.bfloat16)
-                hots.append(
-                    jnp.concatenate([jnp.where(s == low, one, zero) for s in steps], axis=0)
-                )
-            source = source_ref[view * sources + k]
-            table = jnp.concatenate(
-                [
-                    pool_ref[h * LOW // share, source, :, h * LOW % share : h * LOW % share + LOW]
-                    for h in range(high)
-                ],
-                axis=0,
-            )
-            found = jnp.dot(
-                table, jnp.concatenate(hots, axis=1), preferred_element_type=jnp.float32
-            )
-            for q in range(2):
+            usable = idx_ref[view, k] >= 0
+            low_ref[k] = jnp.where(usable, idx_ref[view, k] & (LOW - 1), -1).astype(jnp.float32)
+            live = live + jnp.where(usable, 1.0, 0.0)
+        scale_ref[...] = 0.5 / jnp.maximum(live, 1.0)
+
+        def one_pair(pair, carry):
+            total = [None] * kinds
+            for k in range(sources):
+                hots, rows = [], []
+                for q in range(2):
+                    rows.append(idx_ref[view, k, pl.ds(2 * pair + q, 1), :])
+                    low = low_ref[k, pl.ds(2 * pair + q, 1), :]
+                    low = jnp.broadcast_to(low, (16, columns)).astype(jnp.bfloat16)
+                    low = jnp.concatenate([low] * (LOW // 16), axis=0)
+                    hots.append(jnp.where(count == low, one, zero))
+                row = jnp.concatenate(rows, axis=1)
+                row = jnp.broadcast_to(row, (groups, 2 * columns))
                 bits = []
                 width = LOW
                 while width < LOW * high:
-                    bits.append((highs[q] & width) != 0)
+                    bits.append((row & width) != 0)
                     width *= 2
+                found = jnp.dot(
+                    table_ref[source_ref[view * sources + k]],
+                    jnp.concatenate(hots, axis=1),
+                    preferred_element_type=jnp.float32,
+                )
                 for t in range(kinds):
+                    first = t * high * groups
                     parts = [
-                        found[
-                            h * chans + t * groups : h * chans + (t + 1) * groups,
-                            q * columns : (q + 1) * columns,
-                        ]
-                        for h in range(high)
+                        found[first + h * groups : first + (h + 1) * groups] for h in range(high)
                     ]
                     for bit in bits:
                         parts = [
                             jnp.where(bit, parts[2 * i + 1], parts[2 * i])
                             for i in range(len(parts) // 2)
                         ]
-                    total[q][t] = parts[0] if k == 0 else total[q][t] + parts[0]
-        cost = []
-        for q in range(2):
+                    total[t] = parts[0] if k == 0 else total[t] + parts[0]
             summed = None
             for t in range(kinds):
-                own = own_ref[0, t * groups : (t + 1) * groups, q * columns : (q + 1) * columns]
-                term = total[q][t] * own
+                term = total[t] * own_ref[view, t * groups : (t + 1) * groups, :]
                 summed = term if summed is None else summed + term
-            cost.append(summed * scale_ref[pl.ds(2 * pair + q, 1), :])
-        start = pl.multiple_of(pair * 2 * groups, 2 * groups)
-        out_ref[0, pl.ds(start, 2 * groups), :] = jnp.concatenate(cost, axis=0).astype(jnp.bfloat16)
+            cost = [
+                summed[:, q * columns : (q + 1) * columns]
+                * scale_ref[pl.ds(2 * pair + q, 1), :]
+                for q in range(2)
+            ]
+            start = pl.multiple_of(pair * (2 * groups) + rim, 2 * groups)
+            cost_ref[view, pl.ds(start, 2 * groups), :] = jnp.concatenate(cost, axis=0).astype(
+                jnp.bfloat16
+            )
+            return carry
+
+        lax.fori_loop(0, lines // 2, one_pair, 0)
+
+        @pl.when(view == 0)
+        def _():
+            pl.semaphore_wait(barrier, shares - 1)
+
+        for o in range(1, shares):
+            slab_copy(o, view).start()
+        start = pl.multiple_of(depth * inner, inner)
+        slabs_ref[depth, view] = cost_ref[view, pl.ds(start, slab), :]
         return carry
 
-    lax.fori_loop(0, pairs, one_pair, 0)
-
-
-def conv_kernel(planes, groups, rows, slab_ref, band_ref, out_ref):
+    lax.fori_loop(0, views, one_view, 0)
+    for view in range(views):
+        for o in range(1, shares):
+            came = lax.rem(depth - o + shares, shares)
+            arrived = slabs_ref.at[came, view]
+            pltpu.make_async_remote_copy(
+                src_ref=arrived,
+                dst_ref=arrived,
+                send_sem=send_sem.at[o - 1, view],
+                recv_sem=recv_sem.at[o - 1, view],
+                device_id=(view_here, came),
+                device_id_type=pl.DeviceIdType.MESH,
+            ).wait_recv()
+    for view in range(views):
+        for o in range(1, shares):
+            slab_copy(o, view).wait_send()
+
+
+def conv_kernel(planes, groups, rows, edge, slab_ref, taps_ref, out_ref, band_ref):
     shares = slab_ref.shape[0]
     columns = slab_ref.shape[-1]
-    height = slab_ref.shape[2] // (planes + 2)
+    height = slab_ref.shape[2] // (planes + 2 * edge)
     out_rows = groups * rows
+
+    @pl.when(pl.program_id(0) == 0)
+    def _():
+        size = 3 * out_rows
+        mix = 3 * groups
+
+        def places(shape, axis):
+            return lax.broadcasted_iota(jnp.int32, shape, axis)
+
+        def log(n):
+            return n.bit_length() - 1
+
+        spread = (places((size, mix), 0) >> log(rows)) == places((size, mix), 1)
+        spread = jnp.where(spread, 1.0, 0.0)
+        into, outof = places((mix, size), 0), places((mix, size), 1)
+        gather = ((outof >> log(out_rows)) == (into >> log(groups))) & (
+            (outof & (groups - 1)) == (into & (groups - 1))
+        )
+        gather = jnp.where(gather, 1.0, 0.0)
+        apart = ((places((size, size), 1) >> log(groups)) & (rows - 1)) - (
+            places((size, size), 0) & (rows - 1)
+        )
+        band = jnp.zeros((size, size), jnp.float32)
+        for b in range(3):
+            part = jnp.dot(spread, taps_ref[b], preferred_element_type=jnp.float32)
+            part = jnp.dot(part, gather, preferred_element_type=jnp.float32)
+            band = jnp.where(apart == b - 1, part, band)
+        band_ref[...] = band.astype(jnp.bfloat16)
+
     lane = lax.broadcasted_iota(jnp.int32, (out_rows, columns), 1)
     for first in range(0, planes, 2):
         block = jnp.concatenate(
             [
                 jnp.concatenate(
-                    [slab_ref[s, 0, p * height : (p + 3) * height, :] for s in range(shares)],
+                    [
+                        slab_ref[s, 0, (p + a) * height : (p + a + 1) * height, :]
+                        for a in range(3)
+                        for s in range(shares)
+                    ],
                     axis=0,
                 )
-                for p in (first, first + 1)
+                for p in (first + edge - 1, first + edge)
             ],
             axis=1,
         )
@@ -262,66 +373,40 @@
         own = jnp.concatenate([own, own], axis=2)
     idx = warp_idx.reshape(views, sources, planes * row_count, columns)
 
-    cost = pl.pallas_call(
-        functools.partial(cost_kernel, sources, high, kinds, groups),
-        grid_spec=pltpu.PrefetchScalarGridSpec(
-            num_scalar_prefetch=1,
-            grid=(views,),
-            in_specs=[
-                pl.BlockSpec((1, sources, planes * row_count, columns), lambda v, s: (v, 0, 0, 0)),
-                pl.BlockSpec(pool.shape, lambda v, s: (0, 0, 0, 0)),
-                pl.BlockSpec((1,) + own.shape[1:], lambda v, s: (v, 0, 0)),
-            ],
-            out_specs=pl.BlockSpec(
-                (1, planes * row_count * groups, columns), lambda v, s: (v, 0, 0)
-            ),
-            scratch_shapes=[
-                pltpu.VMEM((sources, planes * row_count, columns), jnp.float32),
-                pltpu.VMEM((planes * row_count, columns), jnp.float32),
-            ],
-        ),
-        out_shape=jax.ShapeDtypeStruct(
-            (views, planes * row_count * groups, columns), jnp.bfloat16
-        ),
-        compiler_params=pltpu.CompilerParams(vmem_limit_bytes=40 * 1024 * 1024),
-    )(view_lists.reshape(-1), idx, pool, own)
-
     height = row_count * groups
     slab_planes = planes // depth_count
-    padded = jnp.pad(cost, ((0, 0), (height, height), (0, 0)))
-    slabs = jnp.stack(
-        [
-            lax.slice_in_dim(
-                padded, t * slab_planes * height, ((t + 1) * slab_planes + 2) * height, axis=1
-            )
-            for t in range(depth_count)
-        ]
-    )
-    slabs = lax.all_to_all(slabs, "depth", split_axis=0, concat_axis=0, tiled=True)
-
-    place = np.zeros((rows, depth_count, row_count, 3), np.float32)
-    for i in range(rows):
-        for b in range(3):
-            j = i + b - 1
-            if 0 <= j < rows:
-                place[i, j // row_count, j % row_count, b] = 1.0
-    taps = conv_weight.reshape(3, 3, 3, groups, groups)
-    band = jnp.einsum(
-        "abegh,isrb->ehisarg",
-        taps,
-        jnp.asarray(place, jnp.bfloat16),
-        preferred_element_type=jnp.float32,
-    ).astype(jnp.bfloat16)
-    band = band.reshape(3 * groups * rows, depth_count * 3 * height)
+    edge = max(1, 16 // height)
+    slab = (slab_planes + 2 * edge) * height
+    slabs = pl.pallas_call(
+        functools.partial(cost_kernel, kinds, groups, slab_planes * height),
+        out_shape=jax.ShapeDtypeStruct((depth_count, views, slab, columns), jnp.bfloat16),
+        in_specs=[pl.BlockSpec(memory_space=pltpu.SMEM)]
+        + [pl.BlockSpec(memory_space=pltpu.VMEM)] * 3,
+        out_specs=pl.BlockSpec(memory_space=pltpu.VMEM),
+        scratch_shapes=[
+            pltpu.VMEM((views, (planes + 2 * edge) * height, columns), jnp.bfloat16),
+            pltpu.VMEM((view_count * asked, high * channels, LOW), jnp.bfloat16),
+            pltpu.VMEM((sources, planes * row_count, columns), jnp.float32),
+            pltpu.VMEM((planes * row_count, columns), jnp.float32),
+            pltpu.SemaphoreType.DMA((depth_count - 1, views)),
+            pltpu.SemaphoreType.DMA((depth_count - 1, views)),
+        ],
+        compiler_params=pltpu.CompilerParams(
+            collective_id=1, has_side_effects=True, vmem_limit_bytes=40 * 1024 * 1024
+        ),
+    )(view_lists.reshape(-1), idx, pool, own)
+
+    taps = conv_weight.reshape(3, 3, 3, groups, groups).transpose(1, 2, 4, 0, 3)
+    taps = taps.reshape(3, 3 * groups, 3 * groups).astype(jnp.float32)
 
     return pl.pallas_call(
-        functools.partial(conv_kernel, slab_planes, groups, rows),
+        functools.partial(conv_kernel, slab_planes, groups, rows, edge),
         grid=(views,),
         in_specs=[
             pl.BlockSpec(
-                (depth_count, 1, (slab_planes + 2) * height, columns), lambda v: (0, v, 0, 0)
+                (depth_count, 1, slab, columns), lambda v: (0, v, 0, 0)
             ),
-            pl.BlockSpec(band.shape, lambda v: (0, 0)),
+            pl.BlockSpec(taps.shape, lambda v: (0, 0, 0)),
         ],
         out_specs=pl.BlockSpec(
             (1, groups, slab_planes, rows, columns), lambda v: (v, 0, 0, 0, 0)
@@ -329,8 +414,9 @@
         out_shape=jax.ShapeDtypeStruct(
             (views, groups, slab_planes, rows, columns), jnp.bfloat16
         ),
+        scratch_shapes=[pltpu.VMEM((3 * groups * rows, 3 * groups * rows), jnp.bfloat16)],
         compiler_params=pltpu.CompilerParams(vmem_limit_bytes=32 * 1024 * 1024),
-    )(slabs, band)
+    )(slabs, taps)
 
 
 def solution(mesh):

time: 144 us -> 101 us (0.70)
  Pallas kernels: 120 us -> 94.9 us
  waiting for transfers between devices: 8.76 us -> 0 us
  starting transfers between devices: 3.72 us -> 0 us
  local copies, waits for them, and re-layouts: 7.52 us -> 5.3 us
    pallas_call x2, Pallas kernels: 102 us -> 77 us  [the longest x1 74.1 us: on_device(): pl.pallas_call(functools.partial(cost_kernel, kinds, groups, slab_planes...]
    all_to_all x1 -> x0, waiting for transfers between devices: 8.76 us -> none  [on_device(): lax.all_to_all(slabs, 'depth', split_axis=0, concat_axis=0, tiled=True)]
    all_to_all x1 -> x0, starting transfers between devices: 3.72 us -> none  [on_device(): lax.all_to_all(slabs, 'depth', split_axis=0, concat_axis=0, tiled=True)]
    unnamed x12 -> x10, local copies, waits for them, and re-layouts: 4.12 us -> 4.13 us
  transfers between devices with their start and end apart: 1 -> 0, of which waited for: 1 -> 0; matrix products, arithmetic and copies ran while one was open for 2% -> 0% of each run, Pallas kernels for 0% -> 0%
where the time goes in v5:
time: 101 us
  Pallas kernels  94.9 us (94%)
  local copies, waits for them, and re-layouts  5.3 us (5%)
    pallas_call x1, Pallas kernels, on_device(): pl.pallas_call(functools.partial(cost_kernel, kinds, groups, slab_planes...  74.1 us
    pallas_call x1, Pallas kernels, on_device(): pl.pallas_call(functools.partial(fetch_kernel, asked), out_shape=jax.Shap...  17.9 us
    unnamed x10, local copies, waits for them, and re-layouts  4.13 us
    pallas_call x1, Pallas kernels, on_device(): pl.pallas_call(functools.partial(conv_kernel, slab_planes, groups, rows,...  2.93 us

profile of v5, /device:TPU:1, one launch (start us, length us, event | category | flops | bytes accessed | tf_op | source)
XLA Modules:
  0.0 101.1 jit_solution(4934966686030593074)
XLA Ops:
  0.0 0.8 dynamic-slice_convert_fusion
  0.9 0.8 copy.10
  1.7 0.1 reshape.23.ask_ref
  1.8 0.0 copy-start.1
  1.8 0.9 copy-done.1
  2.8 0.0 copy-start.2
  2.8 0.7 copy-done.2
  3.5 17.9 %shard_map.64.pool_ref = bf16[4,16,32,256]{3,2,1,0:T(8,128)(2,1)S(1)} custom-call(s32[128]{0:T(128)S(1)} %reshape.23.ask_ref, bf16[3,32,1024]{2,1,0:T(8,128)(2,1)S(1)} %bitcast.15, bf16[32,32]{1,0:T(8,128)(2,1)S(1)} %copy-done.2), custom_call_target="tpu_custom_call" | custom-call | tf_op jit(solution)/shard_map/pallas_call | solution.py:343
  21.4 0.8 reshape.21.source_ref
  22.1 0.0 copy-start
  22.1 1.5 %copy-done = s32[3,10,64,2,128]{4,3,2,1,0:T(2,128)S(1)} copy-done((s32[3,10,64,2,128]{4,3,2,1,0:T(2,128)S(1)}, s32[3,10,64,2,128]{4,3,2,1,0:T(2,128)}, u32[]{:S(2)}) %copy-start) | copy-done | bytes 1966104
  23.7 0.0 copy-start.3
  23.7 74.1 %shard_map.65.slab_ref = bf16[4,3,288,128]{3,2,1,0:T(8,128)(2,1)S(1)} custom-call(s32[30]{0:T(128)S(1)} %reshape.21.source_ref, s32[3,10,128,128]{3,2,1,0:T(8,128)S(1)} %bitcast.13, bf16[4,16,32,256]{3,2,1,0:T(8,128)(2,1)S(1)} %shard_map.64.pool_ref, f32[3,32,256]{2,1,0:T(8,128)S(1)} %bitcast.14), custom_call_target="tpu_custom_call" | custom-call | tf_op jit(solution)/shard_map/pallas_call | solution.py:380
  97.8 0.0 copy-done.3
  97.8 0.1 copy.12
  98.0 0.1 copy.13
  98.1 0.1 reshape.25.taps_ref
  98.2 2.9 %shard_map.66 = bf16[3,8,16,8,128]{4,3,2,1,0:T(8,128)(2,1)} custom-call(bf16[4,3,288,128]{3,2,1,0:T(8,128)(2,1)S(1)} %shard_map.65.slab_ref, f32[3,24,24]{2,1,0:T(8,128)S(1)} %reshape.25.taps_ref), custom_call_target="tpu_custom_call" | custom-call | tf_op jit(solution)/shard_map/pallas_call | solution.py:402
  (3 shorter events, 0.1 us)
Async XLA Ops:
  1.8 0.9 copy-start.1
  2.8 0.7 copy-start.2
  22.1 1.5 %copy-start = (s32[3,10,64,2,128]{4,3,2,1,0:T(2,128)S(1)}, s32[3,10,64,2,128]{4,3,2,1,0:T(2,128)}, u32[]{:S(2)}) copy-start(s32[3,10,64,2,128]{4,3,2,1,0:T(2,128)} %param.9) | copy-start | bytes 5898244
  23.7 74.1 %copy-start.3 = (bf16[27,8,8]{0,2,1:T(8,128)(2,1)S(1)}, bf16[27,8,8]{0,2,1:T(8,128)(2,1)}, u32[]{:S(2)}) copy-start(bf16[27,8,8]{0,2,1:T(8,128)(2,1)} %param.10) | copy-start | bytes 10372

commit v6 on v5

--- a/solution.py
+++ b/solution.py
@@ -12,7 +12,7 @@
 
 
 def fetch_kernel(
-    asked, ask_ref, tiles_ref, order_ref, pool_ref, stage, send_v, recv_v, send_x, recv_x, send_c, recv_c
+    asked, ask_ref, tiles_ref, order_ref, pool_ref, own_ref, stage, send_v, recv_v, send_x, recv_x, send_c, recv_c
 ):
     views = lax.axis_size("view")
     shares = lax.axis_size("depth")
@@ -55,6 +55,11 @@
             tile = tiles_ref[ask_ref[(owner * views + view) * asked + c], :, pl.ds(start, width)]
             moved = jnp.dot(order_ref[...], tile, preferred_element_type=jnp.float32)
             stage[owner, c] = moved.astype(jnp.bfloat16)
+    for tile in range(tiles_ref.shape[0]):
+        part = tiles_ref[tile, :, pl.ds(start, width)]
+        part = jnp.dot(order_ref[...], part, preferred_element_type=jnp.float32)
+        for i in range(own_ref.shape[-1] // width):
+            own_ref[tile, :, i * width : (i + 1) * width] = part
     pl.semaphore_wait(barrier, len(peers))
 
     over_view = []
@@ -230,7 +235,7 @@
             )
             return carry
 
-        lax.fori_loop(0, lines // 2, one_pair, 0)
+        lax.fori_loop(0, lines // 2, one_pair, 0, unroll=4)
 
         @pl.when(view == 0)
         def _():
@@ -324,7 +329,6 @@
 
 
 def on_device(features, view_lists, requests, warp_idx, conv_weight):
-    depth_here = lax.axis_index("depth")
     view_count = lax.axis_size("view")
     depth_count = lax.axis_size("depth")
     views, pixels, channels = features.shape
@@ -340,17 +344,20 @@
     order = np.zeros((channels, channels), np.float32)
     for c in range(channels):
         order[(c % kinds) * groups + c // kinds, c] = 1.0
-    pool = pl.pallas_call(
+    pool, own = pl.pallas_call(
         functools.partial(fetch_kernel, asked),
-        out_shape=jax.ShapeDtypeStruct(
-            (depth_count, view_count * asked, channels, share), jnp.bfloat16
+        out_shape=(
+            jax.ShapeDtypeStruct(
+                (depth_count, view_count * asked, channels, share), jnp.bfloat16
+            ),
+            jax.ShapeDtypeStruct((views, channels, 2 * columns), jnp.float32),
         ),
         in_specs=[
             pl.BlockSpec(memory_space=pltpu.SMEM),
             pl.BlockSpec(memory_space=pltpu.VMEM),
             pl.BlockSpec(memory_space=pltpu.VMEM),
         ],
-        out_specs=pl.BlockSpec(memory_space=pltpu.VMEM),
+        out_specs=(pl.BlockSpec(memory_space=pltpu.VMEM),) * 2,
         scratch_shapes=[
             pltpu.VMEM((view_count, asked, channels, share), jnp.bfloat16),
             pltpu.SemaphoreType.DMA((view_count - 1,)),
@@ -365,12 +372,6 @@
         ),
     )(requests.reshape(-1), features.transpose(0, 2, 1), jnp.asarray(order, jnp.bfloat16))
 
-    own_pixels = row_count * columns
-    own = lax.dynamic_slice_in_dim(features, depth_here * own_pixels, own_pixels, 1)
-    own = own.reshape(views, own_pixels, groups, kinds).transpose(0, 3, 2, 1)
-    own = own.reshape(views, channels, own_pixels).astype(jnp.float32)
-    if row_count == 1:
-        own = jnp.concatenate([own, own], axis=2)
     idx = warp_idx.reshape(views, sources, planes * row_count, columns)
 
     height = row_count * groups

time: 101 us -> 74.6 us (0.74)
  Pallas kernels: 94.9 us -> 69 us
    pallas_call x1, Pallas kernels: 74.1 us -> 48.2 us  [on_device(): pl.pallas_call(functools.partial(cost_kernel, kinds, groups, slab_planes...]
where the time goes in v6:
time: 74.6 us; the launch traced here: 74.4 us
  Pallas kernels  69 us (92%)
  local copies, waits for them, and re-layouts  5.25 us (7%)
    pallas_call x1, Pallas kernels, on_device(): pl.pallas_call(functools.partial(cost_kernel, kinds, groups, slab_planes...  48.2 us
    pallas_call x1, Pallas kernels, on_device(): pl.pallas_call(functools.partial(fetch_kernel, asked), out_shape=(jax.Sha...  17.9 us
    unnamed x10, local copies, waits for them, and re-layouts  4.12 us
    pallas_call x1, Pallas kernels, on_device(): pl.pallas_call(functools.partial(conv_kernel, slab_planes, groups, rows,...  2.93 us

profile of v6, /device:TPU:1, one launch (start us, length us, event | category | flops | bytes accessed | tf_op | source)
XLA Modules:
  0.0 74.4 jit_solution(16391213672846215939)
XLA Ops:
  0.0 0.8 %copy.9 = s32[8,8,2]{2,1,0:T(8,128)S(1)} copy(s32[8,8,2]{1,2,0:T(2,128)} %param.8) | data formatting | bytes 1024 | tf_op args[2]
  0.8 0.1 reshape.17.ask_ref
  1.0 0.0 copy-start.1
  1.0 0.9 %copy-done.1 = bf16[3,1024,32]{1,2,0:T(8,128)(2,1)S(1)} copy-done((bf16[3,1024,32]{1,2,0:T(8,128)(2,1)S(1)}, bf16[3,1024,32]{1,2,0:T(8,128)(2,1)}, u32[]{:S(2)}) %copy-start.1) | copy-done | bytes 196632
  1.9 0.0 copy-start.2
  1.9 0.7 copy-done.2
  2.6 17.9 %shard_map.64 = (bf16[4,16,32,256]{3,2,1,0:T(8,128)(2,1)S(1)}, f32[3,32,256]{2,1,0:T(8,128)S(1)}) custom-call(s32[128]{0:T(128)S(1)} %reshape.17.ask_ref, bf16[3,32,1024]{2,1,0:T(8,128)(2,1)S(1)} %bitcast.7, bf16[32,32]{1,0:T(8,128)(2,1)S(1)} %copy-done.2), custom_call_target="tpu_custom_call" | custom-call | tf_op jit(solution)/shard_map/pallas_call | solution.py:347
  20.5 0.8 %reshape.15.source_ref = s32[30]{0:T(128)S(1)} reshape(s32[3,10]{1,0:T(4,128)} %param.7) | data formatting | bytes 240 | tf_op jit(solution)/shard_map/reshape | solution.py:398
  21.3 0.0 copy-start
  21.3 1.5 %copy-done = s32[3,10,64,2,128]{4,3,2,1,0:T(2,128)S(1)} copy-done((s32[3,10,64,2,128]{4,3,2,1,0:T(2,128)S(1)}, s32[3,10,64,2,128]{4,3,2,1,0:T(2,128)}, u32[]{:S(2)}) %copy-start) | copy-done | bytes 1966104
  22.8 0.0 copy-start.3
  22.8 48.2 %shard_map.65.slab_ref = bf16[4,3,288,128]{3,2,1,0:T(8,128)(2,1)S(1)} custom-call(s32[30]{0:T(128)S(1)} %reshape.15.source_ref, s32[3,10,128,128]{3,2,1,0:T(8,128)S(1)} %bitcast.6, bf16[4,16,32,256]{3,2,1,0:T(8,128)(2,1)S(1)} %get-tuple-element.7.pool_ref, f32[3,32,256]{2,1,0:T(8,128)S(1)} %get-tuple-element.8.own_ref), custom_call_target="tpu_custom_call" | custom-call | tf_op jit(solution)/shard_map/pallas_call | solution.py:381
  71.0 0.0 copy-done.3
  71.0 0.1 copy.10
  71.2 0.1 copy.11
  71.3 0.1 reshape.18.taps_ref
  71.4 2.9 %shard_map.66 = bf16[3,8,16,8,128]{4,3,2,1,0:T(8,128)(2,1)} custom-call(bf16[4,3,288,128]{3,2,1,0:T(8,128)(2,1)S(1)} %shard_map.65.slab_ref, f32[3,24,24]{2,1,0:T(8,128)S(1)} %reshape.18.taps_ref), custom_call_target="tpu_custom_call" | custom-call | tf_op jit(solution)/shard_map/pallas_call | solution.py:403
  (1 shorter events, 0.0 us)
Async XLA Ops:
  1.0 0.9 %copy-start.1 = (bf16[3,1024,32]{1,2,0:T(8,128)(2,1)S(1)}, bf16[3,1024,32]{1,2,0:T(8,128)(2,1)}, u32[]{:S(2)}) copy-start(bf16[3,1024,32]{1,2,0:T(8,128)(2,1)} %param.6) | copy-start | bytes 589828
  1.9 0.7 copy-start.2
  21.3 1.5 %copy-start = (s32[3,10,64,2,128]{4,3,2,1,0:T(2,128)S(1)}, s32[3,10,64,2,128]{4,3,2,1,0:T(2,128)}, u32[]{:S(2)}) copy-start(s32[3,10,64,2,128]{4,3,2,1,0:T(2,128)} %param.9) | copy-start | bytes 5898244
  22.8 48.2 %copy-start.3 = (bf16[27,8,8]{0,2,1:T(8,128)(2,1)S(1)}, bf16[27,8,8]{0,2,1:T(8,128)(2,1)}, u32[]{:S(2)}) copy-start(bf16[27,8,8]{0,2,1:T(8,128)(2,1)} %param.10) | copy-start | bytes 10372

commit v7 on v6

--- a/solution.py
+++ b/solution.py
@@ -44,8 +44,7 @@
 
     barrier = pltpu.get_barrier_semaphore()
     peers = [(at_view(o), depth) for o in range(1, views)]
-    peers += [(view, at_line(o)) for o in range(1, lines)]
-    peers += [(view, other)]
+    peers += [(view, lax.rem(depth + o, shares)) for o in range(1, shares)]
     for peer in peers:
         pl.semaphore_signal(barrier, inc=1, device_id=peer, device_id_type=pl.DeviceIdType.MESH)
 
@@ -134,15 +133,6 @@
     depth = lax.axis_index("depth")
     slab = slabs_ref.shape[2]
     rim = (slab - inner) // 2
-
-    barrier = pltpu.get_barrier_semaphore()
-    for o in range(1, shares):
-        pl.semaphore_signal(
-            barrier,
-            inc=1,
-            device_id=(view_here, lax.rem(depth + o, shares)),
-            device_id_type=pl.DeviceIdType.MESH,
-        )
 
     def one_table(slot, carry):
         parts = [
@@ -235,11 +225,7 @@
             )
             return carry
 
-        lax.fori_loop(0, lines // 2, one_pair, 0, unroll=4)
-
-        @pl.when(view == 0)
-        def _():
-            pl.semaphore_wait(barrier, shares - 1)
+        lax.fori_loop(0, lines // 2, one_pair, 0, unroll=min(16, lines // 2))
 
         for o in range(1, shares):
             slab_copy(o, view).start()
@@ -265,6 +251,32 @@
             slab_copy(o, view).wait_send()
 
 
+def fetch_and_cost(
+    asked,
+    kinds,
+    groups,
+    inner,
+    ask_ref,
+    source_ref,
+    tiles_ref,
+    order_ref,
+    far_idx_ref,
+    slabs_ref,
+    idx_ref,
+    idx_sem,
+    pool_ref,
+    own_ref,
+    *scratch,
+):
+    indices = pltpu.make_async_copy(far_idx_ref, idx_ref, idx_sem)
+    indices.start()
+    fetch_kernel(asked, ask_ref, tiles_ref, order_ref, pool_ref, own_ref, *scratch[:7])
+    indices.wait()
+    cost_kernel(
+        kinds, groups, inner, source_ref, idx_ref, pool_ref, own_ref, slabs_ref, *scratch[7:]
+    )
+
+
 def conv_kernel(planes, groups, rows, edge, slab_ref, taps_ref, out_ref, band_ref):
     shares = slab_ref.shape[0]
     columns = slab_ref.shape[-1]
@@ -344,21 +356,27 @@
     order = np.zeros((channels, channels), np.float32)
     for c in range(channels):
         order[(c % kinds) * groups + c // kinds, c] = 1.0
-    pool, own = pl.pallas_call(
-        functools.partial(fetch_kernel, asked),
-        out_shape=(
-            jax.ShapeDtypeStruct(
-                (depth_count, view_count * asked, channels, share), jnp.bfloat16
-            ),
-            jax.ShapeDtypeStruct((views, channels, 2 * columns), jnp.float32),
-        ),
+    idx = warp_idx.reshape(views, sources, planes * row_count, columns)
+    height = row_count * groups
+    slab_planes = planes // depth_count
+    edge = max(1, 16 // height)
+    slab = (slab_planes + 2 * edge) * height
+    slabs = pl.pallas_call(
+        functools.partial(fetch_and_cost, asked, kinds, groups, slab_planes * height),
+        out_shape=jax.ShapeDtypeStruct((depth_count, views, slab, columns), jnp.bfloat16),
         in_specs=[
+            pl.BlockSpec(memory_space=pltpu.SMEM),
             pl.BlockSpec(memory_space=pltpu.SMEM),
             pl.BlockSpec(memory_space=pltpu.VMEM),
             pl.BlockSpec(memory_space=pltpu.VMEM),
+            pl.BlockSpec(memory_space=pl.ANY),
         ],
-        out_specs=(pl.BlockSpec(memory_space=pltpu.VMEM),) * 2,
+        out_specs=pl.BlockSpec(memory_space=pltpu.VMEM),
         scratch_shapes=[
+            pltpu.VMEM(idx.shape, jnp.int32),
+            pltpu.SemaphoreType.DMA,
+            pltpu.VMEM((depth_count, view_count * asked, channels, share), jnp.bfloat16),
+            pltpu.VMEM((views, channels, 2 * columns), jnp.float32),
             pltpu.VMEM((view_count, asked, channels, share), jnp.bfloat16),
             pltpu.SemaphoreType.DMA((view_count - 1,)),
             pltpu.SemaphoreType.DMA((view_count - 1,)),
@@ -366,25 +384,6 @@
             pltpu.SemaphoreType.DMA((lines, view_count)),
             pltpu.SemaphoreType.DMA((lines, view_count)),
             pltpu.SemaphoreType.DMA((lines, view_count)),
-        ],
-        compiler_params=pltpu.CompilerParams(
-            collective_id=0, has_side_effects=True, vmem_limit_bytes=16 * 1024 * 1024
-        ),
-    )(requests.reshape(-1), features.transpose(0, 2, 1), jnp.asarray(order, jnp.bfloat16))
-
-    idx = warp_idx.reshape(views, sources, planes * row_count, columns)
-
-    height = row_count * groups
-    slab_planes = planes // depth_count
-    edge = max(1, 16 // height)
-    slab = (slab_planes + 2 * edge) * height
-    slabs = pl.pallas_call(
-        functools.partial(cost_kernel, kinds, groups, slab_planes * height),
-        out_shape=jax.ShapeDtypeStruct((depth_count, views, slab, columns), jnp.bfloat16),
-        in_specs=[pl.BlockSpec(memory_space=pltpu.SMEM)]
-        + [pl.BlockSpec(memory_space=pltpu.VMEM)] * 3,
-        out_specs=pl.BlockSpec(memory_space=pltpu.VMEM),
-        scratch_shapes=[
             pltpu.VMEM((views, (planes + 2 * edge) * height, columns), jnp.bfloat16),
             pltpu.VMEM((view_count * asked, high * channels, LOW), jnp.bfloat16),
             pltpu.VMEM((sources, planes * row_count, columns), jnp.float32),
@@ -393,9 +392,15 @@
             pltpu.SemaphoreType.DMA((depth_count - 1, views)),
         ],
         compiler_params=pltpu.CompilerParams(
-            collective_id=1, has_side_effects=True, vmem_limit_bytes=40 * 1024 * 1024
+            collective_id=0, has_side_effects=True, vmem_limit_bytes=48 * 1024 * 1024
         ),
-    )(view_lists.reshape(-1), idx, pool, own)
+    )(
+        requests.reshape(-1),
+        view_lists.reshape(-1),
+        features.transpose(0, 2, 1),
+        jnp.asarray(order, jnp.bfloat16),
+        idx,
+    )
 
     taps = conv_weight.reshape(3, 3, 3, groups, groups).transpose(1, 2, 4, 0, 3)
     taps = taps.reshape(3, 3 * groups, 3 * groups).astype(jnp.float32)

time: 74.6 us -> 68.2 us (0.914)
  Pallas kernels: 69 us -> 61.8 us
    pallas_call x2 -> x1, Pallas kernels: 66.1 us -> 58.8 us  [on_device(): pl.pallas_call(functools.partial(fetch_and_cost, asked, kinds, groups, sl...]
    unnamed x10 -> x8, local copies, waits for them, and re-layouts: 4.12 us -> 4.83 us
where the time goes in v7:
time: 68.2 us; the launch traced here: 67.8 us
  Pallas kernels  61.8 us (91%)
  local copies, waits for them, and re-layouts  5.95 us (9%)
    pallas_call x1, Pallas kernels, on_device(): pl.pallas_call(functools.partial(fetch_and_cost, asked, kinds, groups, sl...  58.8 us
    unnamed x8, local copies, waits for them, and re-layouts  4.83 us
    pallas_call x1, Pallas kernels, on_device(): pl.pallas_call(functools.partial(conv_kernel, slab_planes, groups, rows,...  2.93 us

profile of v7, /device:TPU:1, one launch (start us, length us, event | category | flops | bytes accessed | tf_op | source)
XLA Modules:
  0.0 67.8 jit_solution(13162550045708741771)
XLA Ops:
  0.0 0.8 %reshape.16.source_ref = s32[30]{0:T(128)S(1)} reshape(s32[3,10]{1,0:T(4,128)} %param.7) | data formatting | bytes 240 | tf_op jit(solution)/shard_map/reshape | solution.py:399
  0.8 0.8 %copy.9 = s32[8,8,2]{2,1,0:T(8,128)S(1)} copy(s32[8,8,2]{1,2,0:T(2,128)} %param.8) | data formatting | bytes 1024 | tf_op args[2]
  1.6 0.1 reshape.15.ask_ref
  1.7 0.9 %copy.10 = bf16[27,8,8]{2,1,0:T(8,128)(2,1)S(1)} copy(bf16[27,8,8]{0,2,1:T(8,128)(2,1)} %param.10) | data formatting | bytes 6912 | tf_op args[4]
  2.6 0.1 copy.11
  2.7 0.1 reshape.18.taps_ref
  2.8 0.0 copy-start
  2.8 1.5 %copy-done = s32[3,10,64,2,128]{4,3,2,1,0:T(2,128)S(1)} copy-done((s32[3,10,64,2,128]{4,3,2,1,0:T(2,128)S(1)}, s32[3,10,64,2,128]{4,3,2,1,0:T(2,128)}, u32[]{:S(2)}) %copy-start) | copy-done | bytes 1966104
  4.4 0.0 copy-start.1
  4.4 0.9 %copy-done.1 = bf16[3,1024,32]{1,2,0:T(8,128)(2,1)S(1)} copy-done((bf16[3,1024,32]{1,2,0:T(8,128)(2,1)S(1)}, bf16[3,1024,32]{1,2,0:T(8,128)(2,1)}, u32[]{:S(2)}) %copy-start.1) | copy-done | bytes 196632
  5.3 0.0 copy-start.2
  5.3 0.7 %copy-done.2 = bf16[32,32]{1,0:T(8,128)(2,1)S(1)} copy-done((bf16[32,32]{1,0:T(8,128)(2,1)S(1)}, bf16[32,32]{1,0:T(8,128)(2,1)}, u32[]{:S(2)}) %copy-start.2) | copy-done | bytes 2072
  6.0 58.8 %shard_map.64.slab_ref = bf16[4,3,288,128]{3,2,1,0:T(8,128)(2,1)S(1)} custom-call(s32[128]{0:T(128)S(1)} %reshape.15.ask_ref, s32[30]{0:T(128)S(1)} %reshape.16.source_ref, bf16[3,32,1024]{2,1,0:T(8,128)(2,1)S(1)} %bitcast.7, bf16[32,32]{1,0:T(8,128)(2,1)S(1)} %copy-done.2, s32[3,10,128,128]{3,2,1,0:T(8,128)S(1)} %bitcast.6), custom_call_target="tpu_custom_call" | custom-call | tf_op jit(solution)/shard_map/pallas_call | solution.py:364
  64.9 2.9 %shard_map.65 = bf16[3,8,16,8,128]{4,3,2,1,0:T(8,128)(2,1)} custom-call(bf16[4,3,288,128]{3,2,1,0:T(8,128)(2,1)S(1)} %shard_map.64.slab_ref, f32[3,24,24]{2,1,0:T(8,128)S(1)} %reshape.18.taps_ref), custom_call_target="tpu_custom_call" | custom-call | tf_op jit(solution)/shard_map/pallas_call | solution.py:408
  (1 shorter events, 0.0 us)
Async XLA Ops:
  2.8 1.5 %copy-start = (s32[3,10,64,2,128]{4,3,2,1,0:T(2,128)S(1)}, s32[3,10,64,2,128]{4,3,2,1,0:T(2,128)}, u32[]{:S(2)}) copy-start(s32[3,10,64,2,128]{4,3,2,1,0:T(2,128)} %param.9) | copy-start | bytes 5898244
  4.4 0.9 %copy-start.1 = (bf16[3,1024,32]{1,2,0:T(8,128)(2,1)S(1)}, bf16[3,1024,32]{1,2,0:T(8,128)(2,1)}, u32[]{:S(2)}) copy-start(bf16[3,1024,32]{1,2,0:T(8,128)(2,1)} %param.6) | copy-start | bytes 589828
  5.3 0.7 %copy-start.2 = (bf16[32,32]{1,0:T(8,128)(2,1)S(1)}, bf16[32,32]{1,0:T(8,128)(2,1)}, u32[]{:S(2)}) copy-start(bf16[32,32]{1,0:T(8,128)(2,1)} %constant.2.clone.order_ref) | copy-start | bytes 6148
